TPU v7x, 32 devices: a whole 2x2x4 slice. The times are simulated.
32 devices in a mesh: tok: 4 (over x, core), con: 2 (over y), out: 4 (over z).
Axes of the slice: x: 2, y: 2, z: 4, core: 2. Of those that a mesh axis runs over, the one named last changes fastest.
Arguments:
- tokens: bfloat16 [2048, 10240], P('tok', ('con', 'out')), may hold values from -200 to 200, as said below
- gain: bfloat16 [10240], P(('con', 'out')), may hold values from 0.099609375 to 1.8984375
- up_weight: bfloat16 [10240, 2, 10240], P('con', None, 'out'), may hold values from -0.0625 to 0.0625
- down_weight: bfloat16 [20480, 10240], P(('con', 'out')), may hold values from -0.0625 to 0.0625
Outputs:
- block_out: bfloat16 [2048, 10240], P('tok', ('con', 'out'))
Inputs may be any that keep to these rules, and one draw needn't show every extreme that they name: `tokens`: activations of the residual stream.
All inputs are finite; a program needn't handle non-finite values.
Results may differ from a plain program's by a relative error of at most 0.028.
Values may be sent and summed in bfloat16 or wider, within the bound.
No kernel may reach another device: no remote copies, remote signals or barrier semaphores. Data moves between devices by JAX's collectives and lax.ppermute only.
A program may use at most 192 MiB of HBM per device.

v0:
```python
import jax
import jax.numpy as jnp
from jax import lax
from jax.sharding import PartitionSpec as P

D = 10240


def normalize(values, totals, gain_row):
    average = totals[0][:, None] / D
    variance = totals[1][:, None] / D - average * average
    return ((values - average) * lax.rsqrt(variance + 1e-05) * gain_row.astype(jnp.float32)).astype(
        jnp.bfloat16
    )


def rounded_product(left, right):
    term = jnp.dot(left, right, preferred_element_type=jnp.float32).astype(jnp.bfloat16)
    term = lax.optimization_barrier(term)
    return term.astype(jnp.float32)


def split_terms(hidden, weights, columns, count):
    product = rounded_product(hidden, weights)
    return jnp.transpose(product.reshape(hidden.shape[0], count, columns), (1, 0, 2))


def local(tokens, gain, up_weight, down_weight):
    columns = tokens.shape[1]
    gathered, gain_row = (
        lax.all_gather(tokens, "out", axis=1, tiled=True),
        lax.all_gather(gain, "out", axis=0, tiled=True),
    )
    values = gathered.astype(jnp.float32)
    totals = lax.psum((jnp.sum(values, axis=1), jnp.sum(values * values, axis=1)), "con")
    normed = normalize(values, totals, gain_row)
    partial_value = jnp.einsum("td,dgh->tgh", normed, up_weight, preferred_element_type=jnp.float32)
    summed = lax.psum_scatter(
        partial_value.astype(jnp.bfloat16), "con", scatter_dimension=1, tiled=True
    ).astype(jnp.float32)
    hidden = jax.nn.gelu(summed, approximate=False).astype(jnp.bfloat16)
    hidden = hidden.reshape(hidden.shape[0], hidden.shape[1] * hidden.shape[2])
    result = lax.psum_scatter(
        split_terms(hidden, down_weight, columns, 1 * lax.axis_size(("con", "out"))).astype(
            jnp.bfloat16
        ),
        ("con", "out"),
        scatter_dimension=0,
        tiled=True,
    ).astype(jnp.float32)
    return result[0].astype(jnp.bfloat16)


def solution(mesh):
    in_specs = (
        P("tok", ("con", "out")),
        P(("con", "out")),
        P("con", None, "out"),
        P(("con", "out"), None),
    )
    out_specs = P("tok", ("con", "out"))
    return jax.shard_map(local, mesh=mesh, in_specs=in_specs, out_specs=out_specs, check_vma=False)
```

profile of v0, /device:TPU:0, one launch (start us, length us, event | category | flops | bytes accessed | tf_op | source)
XLA Modules:
  0.0 460.6 jit_solution(4915268919996056760)
XLA Ops:
  6.5 0.0 all-gather.3.cloned.1.call-start
  6.5 0.7 all-gather.3.cloned.1.call-update
  7.3 0.0 reduce-scatter.3.cloned.1.call-start
  7.3 0.7 reshape.16
  8.0 14.8 %all-gather = bf16[4,1,1280]{2,1,0:T(2,128)(2,1)S(1)} all-gather(bf16[1,1,1280]{2,1,0:T(2,128)(2,1)S(1)} %reshape.16), channel_id=1, replica_groups=mesh['tok'=4,'con'=2,'out'=4] {'out'}, dimensions={0}, use_global_device_ids=true | all-gather | bytes 12800 | tf_op jit(solution)/shard_map/all_gather | solution.py:32
  22.8 86.9 %all-gather.3.cloned.1.call-done = bf16[512,5120]{1,0:T(8,128)(2,1)} async-done(((bf16[512,1280]{1,0:T(8,128)(2,1)}), bf16[512,5120]{1,0:T(8,128)(2,1)}) %all-gather.3.cloned.1.call-update) | async-done | bytes 5242896 | tf_op jit(solution)/shard_map/all_gather | solution.py:31
  109.7 4.1 convert_reduce_fusion
  113.8 4.9 %all-reduce = (f32[512]{0:T(512)S(1)}, f32[512]{0:T(512)S(1)}) all-reduce(f32[512]{0:T(512)S(1)} %get-tuple-element.6, f32[512]{0:T(512)S(1)} %get-tuple-element.5), channel_id=1, replica_groups=mesh['tok'=4,'con'=2,'out'=4] {'con'}, use_global_device_ids=true, to_apply=%region_3.0 | all-reduce | flops 1024 | bytes 8192 | tf_op jit(solution)/shard_map/psum | solution.py:35
  118.7 38.0 %fusion.6 = bf16[512,2,2560]{2,0,1:T(8,128)(2,1)} fusion(bf16[5120,2,2560]{2,1,0:T(2,128)(2,1)} %param.6, bf16[512,5120]{1,0:T(8,128)(2,1)} %all-gather.3.cloned.1.call-done, f32[5120]{0:T(1024)S(1)} %bitcast.23, f32[512]{0:T(512)S(1)} %get-tuple-element.10, f32[512]{0:T(512)S(1)} %get-tuple-element.9), kind=kOutput, calls=%fused_computation.14 | convolution fusion | flops 26859274240 | bytes 62939136 | tf_op jit(solution)/shard_map/td,dgh->tgh/dot_general | solution.py:37
  156.8 0.0 reduce-scatter.3.cloned.1.call-update
  156.8 0.2 reduce-scatter.5.cloned.1.call-start
  157.0 64.0 %reduce-scatter.3.cloned.1.call-done = bf16[512,1,2560]{2,0,1:T(8,128)(2,1)} async-done(((bf16[512,2,2560]{2,0,1:T(8,128)(2,1)}), bf16[512,1,2560]{2,0,1:T(8,128)(2,1)}) %reduce-scatter.3.cloned.1.call-update) | async-done | bytes 2621456 | tf_op jit(solution)/shard_map/reduce_scatter | solution.py:38
  221.0 12.4 %fusion.111 = bf16[512,2560]{1,0:T(8,128)(2,1)S(1)} fusion(bf16[512,1,2560]{2,0,1:T(8,128)(2,1)} %reduce-scatter.3.cloned.1.call-done), kind=kLoop, calls=%fused_computation.50.clone.clone.1 | loop fusion | flops 86507520 | bytes 5242880 | tf_op jit(solution)/shard_map/dot_general | solution.py:18
  233.3 34.0 %convolution_convert_fusion = bf16[512,10240]{1,0:T(8,128)(2,1)} fusion(bf16[2560,10240]{1,0:T(8,128)(2,1)} %param.7, bf16[512,2560]{1,0:T(8,128)(2,1)S(1)} %fusion.111), kind=kOutput, calls=%fused_computation.5 | convolution fusion | flops 26848788480 | bytes 65536000 | tf_op jit(solution)/shard_map/dot_general | solution.py:18
  267.4 8.5 %copy.15 = bf16[64,8,8,1280]{3,2,0,1:T(8,128)(2,1)} copy(bf16[64,8,8,1280]{3,2,1,0:T(8,128)(2,1)} %bitcast.22) | data formatting | bytes 20971520 | tf_op jit(solution)/shard_map/convert_element_type | solution.py:44
  275.9 0.0 reduce-scatter.5.cloned.1.call-update
  275.9 178.2 %reduce-scatter.5.cloned.1.call-done = bf16[1,512,1280]{2,1,0:T(8,128)(2,1)} async-done(((bf16[8,512,1280]{2,1,0:T(8,128)(2,1)}), bf16[1,512,1280]{2,1,0:T(8,128)(2,1)}) %reduce-scatter.5.cloned.1.call-update) | async-done | bytes 1310736 | tf_op jit(solution)/shard_map/reduce_scatter | solution.py:43
  (2 shorter events, 0.0 us)
Async XLA Ops:
  6.5 103.2 %all-gather.3.cloned.1.call-start = ((), (), s32[]{:S(2)}) async-start(), calls=%async_computation.2 | async-start | bytes 6553600 | tf_op jit(solution)/shard_map/all_gather | solution.py:31
  7.3 213.7 %reduce-scatter.3.cloned.1.call-start = ((), (), s32[]{:S(2)}) async-start(), calls=%async_computation.3 | async-start | bytes 7864320 | tf_op jit(solution)/shard_map/reduce_scatter | solution.py:38
  156.8 297.3 %reduce-scatter.5.cloned.1.call-start = ((), (), s32[]{:S(2)}) async-start(), calls=%async_computation.4 | async-start | bytes 11796480 | tf_op jit(solution)/shard_map/reduce_scatter | solution.py:43
Sparse Core Ops, SparseCore 0:
  8.9 100.7 all-gather.2
  156.9 64.0 reduce-scatter.2
  276.0 178.0 reduce-scatter.4
where the time goes:
time: 461 us
  waiting for transfers between devices  330 us (72%)
  matrix products  72 us (16%)
  blocking collectives  19.7 us (4%)
  other arithmetic  16.5 us (4%)
  between operations  13.1 us (3%)
  local copies, waits for them, and re-layouts  9.18 us (2%)
    reduce_scatter x1, waiting for transfers between devices, local(): lax.psum_scatter(split_terms(hidden, down_weight, columns, 1 * lax.axis_s...  178 us
    all_gather x1, waiting for transfers between devices, local(): lax.all_gather(tokens, 'out', axis=1, tiled=True)  86.9 us
    reduce_scatter x1, waiting for transfers between devices, local(): lax.psum_scatter(partial_value.astype(jnp.bfloat16), 'con', scatter_dimen...  64 us
    dot_general x1, matrix products, local(): jnp.einsum('td,dgh->tgh', normed, up_weight, preferred_element_type=jnp.f...  38 us
    dot_general x1, matrix products, rounded_product(): jnp.dot(left, right, preferred_element_type=jnp.float32)  34 us
    all_gather x1, blocking collectives, local(): lax.all_gather(gain, 'out', axis=0, tiled=True)  14.8 us
    dot_general x1, other arithmetic, rounded_product(): jnp.dot(left, right, preferred_element_type=jnp.float32)  12.4 us
  transfers between devices with their start and end apart: 3, of which 3 were waited for; matrix products, arithmetic and copies ran while one was open for 0% of the time, Pallas kernels for 0%

commit v1 on v0

v1 whole, which is shorter than its diff:
```python
import functools

import jax
import jax.numpy as jnp
from jax import lax
from jax.experimental import pallas as pl
from jax.experimental.pallas import tpu as pltpu
from jax.sharding import PartitionSpec as P

D = 10240
CHUNKS = (7, 9)


def order_of(line):
    return (
        [("norm", 0), ("upo", 0, 0), ("upo", 0, 1), ("upw", 0), ("gelu", 0, 0), ("gelu", 0, 1)]
        + [("s", 0, "o"), ("s", 0, "w"), ("norm", 1), ("upo", 1, 0), ("upo", 1, 1)]
        + [("upw", 1), ("gelu", 1, 0), ("gelu", 1, 1)]
        + [("do", 1, 0, 1), ("do", 1, 1, 1), ("do", 1, 2, line - 2)]
        + [("dw", 1, 0, line // 2), ("m", 1, 0)]
        + [("dw", 1, line // 2, line - line // 2)]
        + [("m", 1, k) for k in range(1, line - 1)]
        + [("x", 0), ("sum", 0), ("fin", 1)]
    )


def tile_of(width):
    return next(tile for tile in (512, 256, 128) if width % tile == 0)


def up_kernel(side_ref, left_ref, right_ref, *refs):
    out_ref = refs[-1]
    out_ref[...] = jnp.dot(
        left_ref[...], right_ref[0], preferred_element_type=jnp.float32
    ).astype(out_ref.dtype)


def up_product(normed, weights, side, first, count, tile, dtype, after):
    rows, depth = normed.shape
    return pl.pallas_call(
        up_kernel,
        grid_spec=pltpu.PrefetchScalarGridSpec(
            num_scalar_prefetch=1,
            grid=(count,),
            in_specs=[
                pl.BlockSpec((rows, depth), lambda j, side: (0, 0)),
                pl.BlockSpec((1, depth, tile), lambda j, side: (side[0], 0, first + j)),
            ]
            + [pl.BlockSpec(memory_space=pl.ANY)] * len(after),
            out_specs=pl.BlockSpec((rows, tile), lambda j, side: (0, j)),
        ),
        out_shape=jax.ShapeDtypeStruct((rows, count * tile), dtype),
        compiler_params=pltpu.CompilerParams(vmem_limit_bytes=40 * 2**20),
        cost_estimate=pl.CostEstimate(flops=1000, bytes_accessed=1000, transcendentals=0),
        name="up_product",
    )(side, normed, weights, *after)


def down_kernel(parts, waits, blocks_ref, *refs):
    lefts, right_ref, outs = refs[:parts], refs[parts], refs[parts + 1 + waits :]
    total, begin = None, 0
    for left in lefts:
        depth = left.shape[1]
        term = jnp.dot(
            left[...], right_ref[begin : begin + depth, :], preferred_element_type=jnp.float32
        )
        total = term if total is None else total + term
        begin += depth
    for k, out in enumerate(outs):

        @pl.when(pl.program_id(0) == k)
        def _(out=out):
            out[...] = total.astype(out.dtype)


def down_products(hidden, weights, table, first, count, columns, after=()):
    rows = hidden[0].shape[0]
    if columns % 128:
        whole = jnp.concatenate(hidden, axis=1)
        return [
            jnp.dot(
                whole,
                lax.dynamic_slice_in_dim(weights, table[first + k] * columns, columns, 1),
                preferred_element_type=jnp.float32,
            ).astype(jnp.bfloat16)
            for k in range(count)
        ]
    return pl.pallas_call(
        functools.partial(down_kernel, len(hidden), len(after)),
        grid_spec=pltpu.PrefetchScalarGridSpec(
            num_scalar_prefetch=1,
            grid=(count,),
            in_specs=[pl.BlockSpec(part.shape, lambda j, table: (0, 0)) for part in hidden]
            + [
                pl.BlockSpec(
                    (weights.shape[0], columns), lambda j, table: (0, table[first + j])
                )
            ]
            + [pl.BlockSpec(memory_space=pl.ANY)] * len(after),
            out_specs=[pl.BlockSpec((rows, columns), lambda j, table: (0, 0))] * count,
        ),
        out_shape=[jax.ShapeDtypeStruct((rows, columns), jnp.bfloat16)] * count,
        compiler_params=pltpu.CompilerParams(vmem_limit_bytes=40 * 2**20),
        cost_estimate=pl.CostEstimate(flops=1000, bytes_accessed=1000, transcendentals=0),
        name="down_products",
    )(table, *hidden, weights, *after)


def stacked_kernel(parts, side_ref, *refs):
    lefts, right_ref, out_ref = refs[:parts], refs[parts], refs[-1]
    total, begin = None, 0
    for left in lefts:
        depth = left.shape[1]
        term = jnp.dot(
            left[...], right_ref[begin : begin + depth, :], preferred_element_type=jnp.float32
        )
        total = term if total is None else total + term
        begin += depth
    out_ref[0] = total.astype(out_ref.dtype)


def stacked_products(hidden, weights, side, line, columns, after):
    rows = hidden[0].shape[0]
    if columns % 128:
        table = side[0] * line + jnp.arange(line, dtype=jnp.int32)
        return jnp.stack(down_products(hidden, weights, table, 0, line, columns))
    return pl.pallas_call(
        functools.partial(stacked_kernel, len(hidden)),
        grid_spec=pltpu.PrefetchScalarGridSpec(
            num_scalar_prefetch=1,
            grid=(line,),
            in_specs=[pl.BlockSpec(piece.shape, lambda p, side: (0, 0)) for piece in hidden]
            + [pl.BlockSpec((weights.shape[0], columns), lambda p, side: (0, side[0] * line + p))]
            + [pl.BlockSpec(memory_space=pl.ANY)] * len(after),
            out_specs=pl.BlockSpec((1, rows, columns), lambda p, side: (p, 0, 0)),
        ),
        out_shape=jax.ShapeDtypeStruct((line, rows, columns), jnp.bfloat16),
        compiler_params=pltpu.CompilerParams(vmem_limit_bytes=40 * 2**20),
        cost_estimate=pl.CostEstimate(flops=1000, bytes_accessed=1000, transcendentals=0),
        name="stacked_products",
    )(side, *hidden, weights, *after)


def normalize(values, totals, gain_row):
    average = totals[0][:, None] / D
    variance = totals[1][:, None] / D - average * average
    return ((values - average) * lax.rsqrt(variance + 1e-05) * gain_row).astype(jnp.bfloat16)


def local(tokens, gain, up_weight, down_weight):
    rows, columns = tokens.shape
    line = lax.axis_size("out")
    half, place = lax.axis_index("con"), lax.axis_index("out")
    swap = [(0, 1), (1, 0)]
    wide = lambda x: x.astype(jnp.float32)

    cuts = [rows * sum(CHUNKS[:i]) // sum(CHUNKS) for i in range(len(CHUNKS) + 1)]
    spans = list(zip(cuts[:-1], cuts[1:]))
    gathered = [lax.all_gather(tokens[a:b], "out", axis=1, tiled=True) for a, b in spans]

    values = wide(tokens)
    mine = jnp.stack([jnp.sum(values, axis=1), jnp.sum(values * values, axis=1)])
    shifts = sorted(range(line), key=lambda s: (-min(s, line - s), s))
    row = (place + jnp.array(shifts, jnp.int32)) % line
    table = jnp.concatenate([(1 - half) * line + row, half * line + row])
    here = half.astype(jnp.int32).reshape(1)
    picks = {"o": 1 - here, "w": here}
    table, picks, mine = lax.optimization_barrier((table, picks, mine))
    mine = mine + lax.ppermute(mine, "con", swap)
    mine = jnp.concatenate([mine.reshape(1, 2 * rows), wide(gain).reshape(1, columns)], axis=1)
    around = [mine] + [
        lax.ppermute(mine, "out", [(p, (p + s) % line) for p in range(line)]) for s in range(1, line)
    ]
    totals = sum(part[0, : 2 * rows] for part in around).reshape(2, rows)
    stacked = jnp.concatenate(around, axis=0)[:, 2 * rows :]
    gain_row = jnp.concatenate(
        [lax.dynamic_index_in_dim(stacked, (place - p + line) % line, 0, False) for p in range(line)]
    )
    totals, gain_row = lax.optimization_barrier((totals, gain_row))

    width = up_weight.shape[2]
    tile = tile_of(width)
    tiles = width // tile
    split = [0, (3 * tiles + 4) // 5, tiles]
    weights = lax.optimization_barrier(jnp.transpose(up_weight, (1, 0, 2)))
    last = [weights]
    have = {}

    def run(f, *args):
        out = f(*args, after=tuple(last))
        last[:] = [out[0] if isinstance(out, (list, tuple)) else out]
        return out

    def plain(f, *args):
        last.append(f(*args))
        return last[-1]

    def task(kind, c, k=0, count=0, *awaited):
        last.extend(have[key] for key in awaited)
        a, b = spans[c]
        if kind == "norm":
            have[kind, c] = plain(
                lambda x, t, g: normalize(wide(x), t, g), gathered[c], totals[:, a:b], gain_row
            )
        elif kind == "upo":
            first, count = split[k], split[k + 1] - split[k]
            out = run(
                lambda x, w, after: up_product(
                    x, w, picks["o"], first, count, tile, jnp.bfloat16, after
                ),
                have["norm", c],
                weights,
            )
            have[kind, c, k] = lax.ppermute(out, "con", swap)
        elif kind == "upw":
            have[kind, c] = run(
                lambda x, w, after: up_product(
                    x, w, picks["w"], 0, tiles, tile, jnp.float32, after
                ),
                have["norm", c],
                weights,
            )
        elif kind == "gelu":
            if k:
                have["gelu", c, 0], have["upo", c, 1] = lax.optimization_barrier(
                    (have["gelu", c, 0], have["upo", c, 1])
                )
            have[kind, c, k] = plain(
                lambda x, y: jax.nn.gelu(
                    x[:, split[k] * tile : split[k + 1] * tile] + wide(y), approximate=False
                ).astype(jnp.bfloat16),
                have["upw", c],
                have["upo", c, k],
            )
        elif kind in ("do", "dw"):
            first = k + line * (kind == "dw")
            outs = run(
                lambda h, v, after: down_products(h, v, table, first, count, columns, after),
                [have["gelu", c, 0], have["gelu", c, 1]],
                down_weight,
            )
            for i, out in enumerate(outs):
                have["p" + kind[1], c, k + i] = (
                    lax.ppermute(out, "con", swap) if kind == "do" else out
                )
        elif kind == "s":
            out = run(
                lambda h, v, after: stacked_products(h, v, picks[k], line, columns, after),
                [have["gelu", c, 0], have["gelu", c, 1]],
                down_weight,
            )
            have["s" + k, c] = lax.psum_scatter(out, "out", scatter_dimension=0)
        elif kind == "x":
            have[kind, c] = lax.ppermute(have["so", c], "con", swap)
        elif kind == "sum":
            have["fin", c] = plain(
                lambda x, y: (wide(x) + wide(y)).astype(jnp.bfloat16), have["sw", c], have["x", c]
            )
        elif kind == "m":
            out = plain(
                lambda x, y: (wide(x) + wide(y)).astype(jnp.bfloat16),
                have["pw", c, k],
                have["po", c, k],
            )
            have["z", c, k] = lax.ppermute(
                out, "out", [(p, (p + shifts[k]) % line) for p in range(line)]
            )
        else:
            have[kind, c] = plain(
                lambda *terms: sum(wide(term) for term in terms).astype(jnp.bfloat16),
                have["pw", c, line - 1],
                have["po", c, line - 1],
                *[have["z", c, i] for i in range(line - 1)],
            )

    for word in order_of(line):
        task(*word)
    return jnp.concatenate([have["fin", c] for c in range(len(spans))], axis=0)


def solution(mesh):
    in_specs = (
        P("tok", ("con", "out")),
        P(("con", "out")),
        P("con", None, "out"),
        P(("con", "out"), None),
    )
    out_specs = P("tok", ("con", "out"))
    return jax.shard_map(local, mesh=mesh, in_specs=in_specs, out_specs=out_specs, check_vma=False)
```

time: 461 us -> 297 us (0.64)
  waiting for transfers between devices: 330 us -> 85.2 us
  Pallas kernels: 0 us -> 113 us
  matrix products: 72 us -> 0 us
  local copies, waits for them, and re-layouts: 9.18 us -> 40.3 us
  blocking collectives: 19.7 us -> 0 us
  starting transfers between devices: 0.26 us -> 19 us
  other arithmetic: 16.5 us -> 25.8 us
    reduce_scatter x2, waiting for transfers between devices: 242 us -> 0.02 us  [task(): have['s' + k, c] = lax.psum_scatter(out, 'out', scatter_dimension=0)]
    pallas_call x0 -> x13, Pallas kernels: none -> 113 us  [the longest x6 54.1 us: up_product(): pl.pallas_call(up_kernel, grid_spec=pltpu.PrefetchScalarGridSpec(num_scal...]
    all_gather x1 -> x2, waiting for transfers between devices: 86.9 us -> 2.1 us  [local(): lax.all_gather(tokens[a:b], 'out', axis=1, tiled=True)]
    ppermute x0 -> x16, waiting for transfers between devices: none -> 83 us  [the longest x4 35.6 us: task(): lax.ppermute(out, 'con', swap)]
    dot_general x2 -> x0, matrix products: 72 us -> none  [the longest x1 38 us: local(): jnp.einsum('td,dgh->tgh', normed, up_weight, preferred_element_type=jnp.f...]
    unnamed x1 -> x15, local copies, waits for them, and re-layouts: 0.69 us -> 37.3 us
    convert_element_type x1 -> x11, other arithmetic: 0.02 us -> 23.9 us  [the longest x4 12.7 us: task(): have[kind, c, k] = plain(lambda x, y: jax.nn.gelu(x[:, split[k] * tile:sp...]
    ppermute x0 -> x16, starting transfers between devices: none -> 18.7 us  [the longest x3 6.1 us: local(): lax.ppermute(mine, 'out', [(p, (p + s) % line) for p in range(line)])]
  transfers between devices with their start and end apart: 3 -> 20, of which waited for: 3 -> 11; matrix products, arithmetic and copies ran while one was open for 0% -> 20% of each run, Pallas kernels for 0% -> 38%
where the time goes in v1:
time: 297 us
  Pallas kernels  113 us (38%)
  waiting for transfers between devices  85.2 us (29%)
  local copies, waits for them, and re-layouts  40.3 us (14%)
  other arithmetic  25.8 us (9%)
  starting transfers between devices  19 us (6%)
  between operations  13.5 us (5%)
    pallas_call x6, Pallas kernels, up_product(): pl.pallas_call(up_kernel, grid_spec=pltpu.PrefetchScalarGridSpec(num_scal...  54.1 us
    unnamed x15, local copies, waits for them, and re-layouts  37.3 us
    ppermute x4, waiting for transfers between devices, task(): lax.ppermute(out, 'con', swap)  35.6 us
    pallas_call x5, Pallas kernels, down_products(): pl.pallas_call(functools.partial(down_kernel, len(hidden), len(after)), g...  34.9 us
    ppermute x3, waiting for transfers between devices, task(): lax.ppermute(out, 'out', [(p, (p + shifts[k]) % line) for p in range(line)])  30.4 us
    pallas_call x2, Pallas kernels, stacked_products(): pl.pallas_call(functools.partial(stacked_kernel, len(hidden)), grid_spec=...  23.8 us
    ppermute x4, waiting for transfers between devices, task(): have[kind, c, k] = lax.ppermute(out, 'con', swap)  13 us
    convert_element_type x4, other arithmetic, task(): have[kind, c, k] = plain(lambda x, y: jax.nn.gelu(x[:, split[k] * tile:sp...  12.7 us
  transfers between devices with their start and end apart: 20, of which 11 were waited for; matrix products, arithmetic and copies ran while one was open for 20% of the time, Pallas kernels for 38%

profile of v1, /device:TPU:0, one launch (start us, length us, event | category | flops | bytes accessed | tf_op | source)
XLA Modules:
  0.0 296.5 jit_solution(14468638835110098507)
XLA Ops:
  6.5 2.0 slice.48
  9.3 3.0 %collective-permute-start = (f32[2,512]{1,0:T(2,128)S(1)}, f32[2,512]{1,0:T(2,128)S(1)}, u32[]{:S(2)}, u32[]{:S(2)}) collective-permute-start(f32[2,512]{1,0:T(2,128)S(1)} %pad_maximum_fusion.5), channel_id=1, source_target_pairs={{0,4},{4,0},{1,5},{5,1},{2,6},{6,2},{3,7},{7,3},{8,12},{12,8},{9,1... | collective-permute-start | bytes 12296 | tf_op jit(solution)/shard_map/ppermute | solution.py:169
  12.3 1.6 collective-permute-done
  13.9 2.1 collective-permute-start.1
  16.1 0.9 slice.57
  17.1 35.9 %copy.9 = bf16[5120,2,2560]{2,0,1:T(8,128)(2,1)} copy(bf16[5120,2,2560]{2,1,0:T(2,128)(2,1)} %param.7) | data formatting | bytes 104857600 | tf_op args[2]
  53.0 2.7 collective-permute-start.2
  55.7 1.3 collective-permute-start.3
  57.7 1.6 collective-permute-done.3
  59.5 2.1 all-gather.3.cloned.1.call-done
  61.6 2.5 multiply_convert_fusion.1.left_ref.refs_1_
  64.1 8.2 %up_product.6.refs_0_ = bf16[224,1536]{1,0:T(8,128)(2,1)S(1)} custom-call(s32[1]{0:T(128)S(6)} %sub.42.side_ref, bf16[224,5120]{1,0:T(8,128)(2,1)S(1)} %multiply_convert_fusion.1.left_ref.refs_1_, bf16[2,5120,2560]{2,1,0:T(8,128)(2,1)} %bitcast.15, bf16[2,5120,2560]{2,1,0:T(8,128)(2,1)} %bitcast.16, bf16[224,5120]{1,0:T(8,128)(2,1)S(1)} %multiply_convert_fusion.1.left_ref.refs_1_), custom_call_target="tpu_custom_call" | custom-call | flops 1000 | bytes 1000 | tf_op jit(solution)/shard_map/up_product/pallas_call | solution.py:40
  72.4 1.6 collective-permute-start.4
  74.0 5.5 %up_product.7.refs_0_ = bf16[224,1024]{1,0:T(8,128)(2,1)S(1)} custom-call(s32[1]{0:T(128)S(6)} %sub.42.side_ref, bf16[224,5120]{1,0:T(8,128)(2,1)S(1)} %multiply_convert_fusion.1.left_ref.refs_1_, bf16[2,5120,2560]{2,1,0:T(8,128)(2,1)} %bitcast.17, bf16[224,1536]{1,0:T(8,128)(2,1)S(1)} %up_product.6.refs_0_), custom_call_target="tpu_custom_call" | custom-call | flops 1000 | bytes 1000 | tf_op jit(solution)/shard_map/up_product/pallas_call | solution.py:40
  80.0 12.0 %up_product.8.refs_3_ = f32[224,2560]{1,0:T(8,128)S(1)} custom-call(s32[1]{0:T(128)} %bitcast.side_ref, bf16[224,5120]{1,0:T(8,128)(2,1)S(1)} %multiply_convert_fusion.1.left_ref.refs_1_, bf16[2,5120,2560]{2,1,0:T(8,128)(2,1)} %bitcast.18, bf16[224,1024]{1,0:T(8,128)(2,1)S(1)} %up_product.7.refs_0_), custom_call_target="tpu_custom_call" | custom-call | flops 1000 | bytes 1000 | tf_op jit(solution)/shard_map/up_product/pallas_call | solution.py:40
  92.0 3.1 %fusion.13.refs_0_.refs_4_ = bf16[224,1536]{1,0:T(8,128)(2,1)S(1)} fusion(bf16[224,1536]{1,0:T(8,128)(2,1)S(1)} %collective-permute-done.4, f32[224,2560]{1,0:T(8,128)S(1)} %up_product.8.refs_3_), kind=kLoop, calls=%fused_computation.34 | loop fusion | flops 23052288 | bytes 2752512 | tf_op jit(solution)/shard_map/convert_element_type | solution.py:231
  95.1 4.4 %collective-permute-done.5 = bf16[224,1024]{1,0:T(8,128)(2,1)S(1)} collective-permute-done((bf16[224,1024]{1,0:T(8,128)(2,1)S(1)}, bf16[224,1024]{1,0:T(8,128)(2,1)S(1)}, u32[]{:S(2)}, u32[]{:S(2)}) %collective-permute-start.5) | collective-permute-done | bytes 458784 | tf_op jit(solution)/shard_map/ppermute | solution.py:214
  99.5 2.0 fusion.34.refs_1_.refs_5_
  101.5 12.6 %stacked_products.2.refs_3_ = bf16[4,224,1280]{2,1,0:T(8,128)(2,1)} custom-call(s32[1]{0:T(128)S(6)} %sub.42.side_ref, bf16[224,1536]{1,0:T(8,128)(2,1)S(1)} %fusion.13.refs_0_.refs_4_, bf16[224,1024]{1,0:T(8,128)(2,1)S(1)} %fusion.34.refs_1_.refs_5_, bf16[2560,10240]{1,0:T(8,128)(2,1)} %refs_2_.13, f32[224,2560]{1,0:T(8,128)S(1)} %up_product.8.refs_3_, ...), custom_call_target="tpu_custom_call" | custom-call | flops 1000 | bytes 1000 | tf_op jit(solution)/shard_map/stacked_products/pallas_call | solution.py:127
  114.5 11.2 %stacked_products.3.refs_0_ = bf16[4,224,1280]{2,1,0:T(8,128)(2,1)S(1)} custom-call(s32[1]{0:T(128)} %bitcast.side_ref, bf16[224,1536]{1,0:T(8,128)(2,1)S(1)} %fusion.13.refs_0_.refs_4_, bf16[224,1024]{1,0:T(8,128)(2,1)S(1)} %fusion.34.refs_1_.refs_5_, bf16[2560,10240]{1,0:T(8,128)(2,1)} %refs_2_.13, bf16[4,224,1280]{2,1,0:T(8,128)(2,1)} %stacked_products.2.refs_3_), custom_call_target="tpu_custom_call" | custom-call | flops 1000 | bytes 1000 | tf_op jit(solution)/shard_map/stacked_products/pallas_call | solution.py:127
  125.7 1.4 copy-done
  127.1 3.2 %multiply_convert_fusion.left_ref.refs_1_ = bf16[288,5120]{1,0:T(8,128)(2,1)S(1)} fusion(bf16[288,5120]{1,0:T(8,128)(2,1)} %all-gather.5.cloned.1.call-done, f32[5120]{0:T(1024)} %copy-done.3, f32[288]{0:T(512)S(1)} %add_rsqrt_fusion, f32[288]{0:T(512)S(1)} %get-tuple-element.43), kind=kLoop, calls=%fused_computation.1 | loop fusion | flops 7372800 | bytes 5921024 | tf_op jit(solution)/shard_map/convert_element_type | solution.py:147
  130.3 9.4 %up_product.9.refs_0_ = bf16[288,1536]{1,0:T(8,128)(2,1)} custom-call(s32[1]{0:T(128)S(6)} %sub.42.side_ref, bf16[288,5120]{1,0:T(8,128)(2,1)S(1)} %multiply_convert_fusion.left_ref.refs_1_, bf16[2,5120,2560]{2,1,0:T(8,128)(2,1)} %bitcast.19, bf16[4,224,1280]{2,1,0:T(8,128)(2,1)S(1)} %copy-done.1, bf16[288,5120]{1,0:T(8,128)(2,1)S(1)} %multiply_convert_fusion.left_ref.refs_1_), custom_call_target="tpu_custom_call" | custom-call | flops 1000 | bytes 1000 | tf_op jit(solution)/shard_map/up_product/pallas_call | solution.py:40
  139.7 1.5 collective-permute-start.7
  141.1 6.1 %up_product.10.refs_0_ = bf16[288,1024]{1,0:T(8,128)(2,1)S(1)} custom-call(s32[1]{0:T(128)S(6)} %sub.42.side_ref, bf16[288,5120]{1,0:T(8,128)(2,1)S(1)} %multiply_convert_fusion.left_ref.refs_1_, bf16[2,5120,2560]{2,1,0:T(8,128)(2,1)} %bitcast.20, bf16[288,1536]{1,0:T(8,128)(2,1)} %up_product.9.refs_0_), custom_call_target="tpu_custom_call" | custom-call | flops 1000 | bytes 1000 | tf_op jit(solution)/shard_map/up_product/pallas_call | solution.py:40
  147.3 12.9 %up_product.11.refs_3_ = f32[288,2560]{1,0:T(8,128)S(1)} custom-call(s32[1]{0:T(128)} %bitcast.side_ref, bf16[288,5120]{1,0:T(8,128)(2,1)S(1)} %multiply_convert_fusion.left_ref.refs_1_, bf16[2,5120,2560]{2,1,0:T(8,128)(2,1)} %bitcast.21, bf16[288,1024]{1,0:T(8,128)(2,1)S(1)} %up_product.10.refs_0_), custom_call_target="tpu_custom_call" | custom-call | flops 1000 | bytes 1000 | tf_op jit(solution)/shard_map/up_product/pallas_call | solution.py:40
  160.8 4.9 %fusion.3.refs_0_.refs_4_ = bf16[288,1536]{1,0:T(8,128)(2,1)S(1)} fusion(bf16[288,1536]{1,0:T(8,128)(2,1)} %collective-permute-done.7, f32[288,2560]{1,0:T(8,128)S(1)} %up_product.11.refs_3_), kind=kLoop, calls=%fused_computation.10 | loop fusion | flops 29638656 | bytes 3538944 | tf_op jit(solution)/shard_map/convert_element_type | solution.py:231
  165.7 8.6 %collective-permute-done.8 = bf16[288,1024]{1,0:T(8,128)(2,1)S(1)} collective-permute-done((bf16[288,1024]{1,0:T(8,128)(2,1)S(1)}, bf16[288,1024]{1,0:T(8,128)(2,1)S(1)}, u32[]{:S(2)}, u32[]{:S(2)}) %collective-permute-start.8) | collective-permute-done | bytes 589856 | tf_op jit(solution)/shard_map/ppermute | solution.py:214
  174.4 2.6 fusion.23.refs_1_.refs_5_
  177.0 5.7 %down_products.5.refs_3_ = bf16[288,1280]{1,0:T(8,128)(2,1)S(1)} custom-call(s32[8]{0:T(128)S(1)} %pad_add_fusion.blocks_ref, bf16[288,1536]{1,0:T(8,128)(2,1)S(1)} %fusion.3.refs_0_.refs_4_, bf16[288,1024]{1,0:T(8,128)(2,1)S(1)} %fusion.23.refs_1_.refs_5_, bf16[2560,10240]{1,0:T(8,128)(2,1)} %refs_2_.13, f32[288,2560]{1,0:T(8,128)S(1)} %up_product.11.refs_3_, ...), custom_call_target="tpu_custom_call" | custom-call | flops 1000 | bytes 1000 | tf_op jit(solution)/shard_map/down_products/pallas_call | solution.py:88
  182.7 5.6 %down_products.6.refs_3_ = bf16[288,1280]{1,0:T(8,128)(2,1)S(1)} custom-call(s32[8]{0:T(128)S(1)} %pad_add_fusion.blocks_ref, bf16[288,1536]{1,0:T(8,128)(2,1)S(1)} %fusion.3.refs_0_.refs_4_, bf16[288,1024]{1,0:T(8,128)(2,1)S(1)} %fusion.23.refs_1_.refs_5_, bf16[2560,10240]{1,0:T(8,128)(2,1)} %refs_2_.13, bf16[288,1280]{1,0:T(8,128)(2,1)S(1)} %down_products.5.refs_3_), custom_call_target="tpu_custom_call" | custom-call | flops 1000 | bytes 1000 | tf_op jit(solution)/shard_map/down_products/pallas_call | solution.py:88
  189.0 1.3 collective-permute-start.9
  190.3 8.0 %down_products.7 = (bf16[288,1280]{1,0:T(8,128)(2,1)S(1)}, bf16[288,1280]{1,0:T(8,128)(2,1)S(1)}) custom-call(s32[8]{0:T(128)S(1)} %pad_add_fusion.blocks_ref, bf16[288,1536]{1,0:T(8,128)(2,1)S(1)} %fusion.3.refs_0_.refs_4_, bf16[288,1024]{1,0:T(8,128)(2,1)S(1)} %fusion.23.refs_1_.refs_5_, bf16[2560,10240]{1,0:T(8,128)(2,1)} %refs_2_.13, ...), custom_call_target="tpu_custom_call" | custom-call | flops 1000 | bytes 1000 | tf_op jit(solution)/shard_map/down_products/pallas_call | solution.py:88
  198.3 7.8 %down_products.8 = (bf16[288,1280]{1,0:T(8,128)(2,1)S(1)}, bf16[288,1280]{1,0:T(8,128)(2,1)S(1)}) custom-call(s32[8]{0:T(128)S(1)} %pad_add_fusion.blocks_ref, bf16[288,1536]{1,0:T(8,128)(2,1)S(1)} %fusion.3.refs_0_.refs_4_, bf16[288,1024]{1,0:T(8,128)(2,1)S(1)} %fusion.23.refs_1_.refs_5_, bf16[2560,10240]{1,0:T(8,128)(2,1)} %refs_2_.13, ...), custom_call_target="tpu_custom_call" | custom-call | flops 1000 | bytes 1000 | tf_op jit(solution)/shard_map/down_products/pallas_call | solution.py:88
  206.1 0.9 collective-permute-start.14
  207.1 1.1 collective-permute-start.10
  208.2 1.1 add_convert_fusion.2
  209.3 14.3 %collective-permute-done.9 = bf16[288,1280]{1,0:T(8,128)(2,1)S(1)} collective-permute-done((bf16[288,1280]{1,0:T(8,128)(2,1)S(1)}, bf16[288,1280]{1,0:T(8,128)(2,1)S(1)}, u32[]{:S(2)}, u32[]{:S(2)}) %collective-permute-start.9) | collective-permute-done | bytes 737312 | tf_op jit(solution)/shard_map/ppermute | solution.py:244
  223.8 7.9 %down_products.9 = (bf16[288,1280]{1,0:T(8,128)(2,1)S(1)}, bf16[288,1280]{1,0:T(8,128)(2,1)S(1)}) custom-call(s32[8]{0:T(128)S(1)} %pad_add_fusion.blocks_ref, bf16[288,1536]{1,0:T(8,128)(2,1)S(1)} %fusion.3.refs_0_.refs_4_, bf16[288,1024]{1,0:T(8,128)(2,1)S(1)} %fusion.23.refs_1_.refs_5_, bf16[2560,10240]{1,0:T(8,128)(2,1)} %refs_2_.13, ...), custom_call_target="tpu_custom_call" | custom-call | flops 1000 | bytes 1000 | tf_op jit(solution)/shard_map/down_products/pallas_call | solution.py:88
  231.7 7.7 %collective-permute-done.14 = bf16[288,1280]{1,0:T(8,128)(2,1)S(1)} collective-permute-done((bf16[288,1280]{1,0:T(8,128)(2,1)S(1)}, bf16[288,1280]{1,0:T(8,128)(2,1)S(1)}, u32[]{:S(2)}, u32[]{:S(2)}) %collective-permute-start.14) | collective-permute-done | bytes 737312 | tf_op jit(solution)/shard_map/ppermute | solution.py:244
  239.3 1.0 add_convert_fusion.1
  240.4 1.0 collective-permute-start.15
  241.5 13.6 %collective-permute-done.10 = bf16[288,1280]{1,0:T(8,128)(2,1)S(1)} collective-permute-done((bf16[288,1280]{1,0:T(8,128)(2,1)S(1)}, bf16[288,1280]{1,0:T(8,128)(2,1)S(1)}, u32[]{:S(2)}, u32[]{:S(2)}) %collective-permute-start.10) | collective-permute-done | bytes 737312 | tf_op jit(solution)/shard_map/ppermute | solution.py:244
  255.1 3.5 %collective-permute-done.15 = bf16[288,1280]{1,0:T(8,128)(2,1)} collective-permute-done((bf16[288,1280]{1,0:T(8,128)(2,1)}, bf16[288,1280]{1,0:T(8,128)(2,1)}, u32[]{:S(2)}, u32[]{:S(2)}) %collective-permute-start.15) | collective-permute-done | bytes 737312 | tf_op jit(solution)/shard_map/ppermute | solution.py:265
  258.6 27.0 %collective-permute-done.11 = bf16[288,1280]{1,0:T(8,128)(2,1)} collective-permute-done((bf16[288,1280]{1,0:T(8,128)(2,1)S(1)}, bf16[288,1280]{1,0:T(8,128)(2,1)}, u32[]{:S(2)}, u32[]{:S(2)}) %collective-permute-start.11) | collective-permute-done | bytes 737312 | tf_op jit(solution)/shard_map/ppermute | solution.py:265
  285.6 2.0 add_convert_fusion
  287.6 1.2 fusion.31
  288.9 1.1 pad_maximum_fusion
  (60 shorter events, 4.3 us)
Async XLA Ops:
  6.5 2.1 copy-start.5
  6.5 2.2 copy-start.2
  6.5 5.8 %copy-start.4 = (bf16[1280]{0:T(1024)(128)(2,1)S(1)}, bf16[1280]{0:T(1024)(128)(2,1)}, u32[]{:S(2)}) copy-start(bf16[1280]{0:T(1024)(128)(2,1)} %param.6) | copy-start | bytes 7684
  6.5 55.1 %all-gather.3.cloned.1.call-start = ((), (), s32[]{:S(2)}) async-start(), calls=%async_computation.2 | async-start | bytes 2867200 | tf_op jit(solution)/shard_map/all_gather | solution.py:159
  8.6 118.5 %all-gather.5.cloned.1.call-start = ((), (), s32[]{:S(2)}) async-start(), calls=%async_computation.5 | async-start | bytes 3686400 | tf_op jit(solution)/shard_map/all_gather | solution.py:159
  9.3 4.6 %collective-permute-start = (f32[2,512]{1,0:T(2,128)S(1)}, f32[2,512]{1,0:T(2,128)S(1)}, u32[]{:S(2)}, u32[]{:S(2)}) collective-permute-start(f32[2,512]{1,0:T(2,128)S(1)} %pad_maximum_fusion.5), channel_id=1, source_target_pairs={{0,4},{4,0},{1,5},{5,1},{2,6},{6,2},{3,7},{7,3},{8,12},{12,8},{9,1... | collective-permute-start | bytes 12296 | tf_op jit(solution)/shard_map/ppermute | solution.py:169
  13.9 43.0 %collective-permute-start.1 = (f32[1,2304]{1,0:T(1,128)S(1)}, f32[1,2304]{1,0:T(1,128)S(1)}, u32[]{:S(2)}, u32[]{:S(2)}) collective-permute-start(f32[1,2304]{1,0:T(1,128)S(1)} %constant_dynamic-update-slice_fusion), channel_id=1, source_target_pairs={{0,1},{1,2},{2,3},{3,0},{4,5},{5,6},{6,7},{7,4},{8,9},{9,10},{10,1... | collective-permute-start | bytes 27656 | tf_op jit(solution)/shard_map/ppermute | solution.py:172
  17.0 224.4 %reduce-scatter.5.cloned.1.call-start = ((), (), s32[]{:S(2)}) async-start(), calls=%async_computation.4 | async-start | bytes 2867200 | tf_op jit(solution)/shard_map/reduce_scatter | solution.py:252
  53.0 4.7 %collective-permute-start.2 = (f32[1,2304]{1,0:T(1,128)S(1)}, f32[1,2304]{1,0:T(1,128)S(1)}, u32[]{:S(2)}, u32[]{:S(2)}) collective-permute-start(f32[1,2304]{1,0:T(1,128)S(1)} %constant_dynamic-update-slice_fusion), channel_id=1, source_target_pairs={{0,2},{1,3},{2,0},{3,1},{4,6},{5,7},{6,4},{7,5},{8,10},{9,11},{10,... | collective-permute-start | bytes 27656 | tf_op jit(solution)/shard_map/ppermute | solution.py:172
  55.7 3.7 %collective-permute-start.3 = (f32[1,2304]{1,0:T(1,128)S(1)}, f32[1,2304]{1,0:T(1,128)S(1)}, u32[]{:S(2)}, u32[]{:S(2)}) collective-permute-start(f32[1,2304]{1,0:T(1,128)S(1)} %constant_dynamic-update-slice_fusion), channel_id=1, source_target_pairs={{0,3},{1,0},{2,1},{3,2},{4,7},{5,4},{6,5},{7,6},{8,11},{9,8},{10,9... | collective-permute-start | bytes 27656 | tf_op jit(solution)/shard_map/ppermute | solution.py:172
  59.5 4.7 %copy-start.3 = (f32[5120]{0:T(1024)}, f32[5120]{0:T(1024)S(1)}, u32[]{:S(2)}) copy-start(f32[5120]{0:T(1024)S(1)} %pad_maximum_fusion.4) | copy-start | bytes 61444
  72.4 19.6 %collective-permute-start.4 = (bf16[224,1536]{1,0:T(8,128)(2,1)S(1)}, bf16[224,1536]{1,0:T(8,128)(2,1)S(1)}, u32[]{:S(2)}, u32[]{:S(2)}) collective-permute-start(bf16[224,1536]{1,0:T(8,128)(2,1)S(1)} %up_product.6.refs_0_), channel_id=1, source_target_pairs={{0,4},{4,0},{1,5},{5,1},{2,6},{6,2},{3,7},{7,3},{8,12},{12,8},{9,1... | collective-permute-start | bytes 2064392 | tf_op jit(solution)/shard_map/ppermute | solution.py:214
  79.5 20.0 %collective-permute-start.5 = (bf16[224,1024]{1,0:T(8,128)(2,1)S(1)}, bf16[224,1024]{1,0:T(8,128)(2,1)S(1)}, u32[]{:S(2)}, u32[]{:S(2)}) collective-permute-start(bf16[224,1024]{1,0:T(8,128)(2,1)S(1)} %up_product.7.refs_0_), channel_id=1, source_target_pairs={{0,4},{4,0},{1,5},{5,1},{2,6},{6,2},{3,7},{7,3},{8,12},{12,8},{9,1... | collective-permute-start | bytes 1376264 | tf_op jit(solution)/shard_map/ppermute | solution.py:214
  114.2 173.5 %reduce-scatter.3.cloned.1.call-start = ((), (), s32[]{:S(2)}) async-start(), calls=%async_computation.3 | async-start | bytes 2867200 | tf_op jit(solution)/shard_map/reduce_scatter | solution.py:252
  125.7 1.4 copy-start
  127.1 3.2 %copy-start.1 = (bf16[4,224,1280]{2,1,0:T(8,128)(2,1)S(1)}, bf16[4,224,1280]{2,1,0:T(8,128)(2,1)}, u32[]{:S(2)}) copy-start(bf16[4,224,1280]{2,1,0:T(8,128)(2,1)} %copy-done) | copy-start | bytes 6881284
  139.7 21.1 %collective-permute-start.7 = (bf16[288,1536]{1,0:T(8,128)(2,1)}, bf16[288,1536]{1,0:T(8,128)(2,1)}, u32[]{:S(2)}, u32[]{:S(2)}) collective-permute-start(bf16[288,1536]{1,0:T(8,128)(2,1)} %up_product.9.refs_0_), channel_id=1, source_target_pairs={{0,4},{4,0},{1,5},{5,1},{2,6},{6,2},{3,7},{7,3},{8,12},{12,8},{9,1... | collective-permute-start | bytes 2654216 | tf_op jit(solution)/shard_map/ppermute | solution.py:214
  160.2 14.2 %collective-permute-start.8 = (bf16[288,1024]{1,0:T(8,128)(2,1)S(1)}, bf16[288,1024]{1,0:T(8,128)(2,1)S(1)}, u32[]{:S(2)}, u32[]{:S(2)}) collective-permute-start(bf16[288,1024]{1,0:T(8,128)(2,1)S(1)} %up_product.10.refs_0_), channel_id=1, source_target_pairs={{0,4},{4,0},{1,5},{5,1},{2,6},{6,2},{3,7},{7,3},{8,12},{12,8},{9,1... | collective-permute-start | bytes 1769480 | tf_op jit(solution)/shard_map/ppermute | solution.py:214
  188.3 20.0 %collective-permute-start.12 = (bf16[288,1280]{1,0:T(8,128)(2,1)S(1)}, bf16[288,1280]{1,0:T(8,128)(2,1)S(1)}, u32[]{:S(2)}, u32[]{:S(2)}) collective-permute-start(bf16[288,1280]{1,0:T(8,128)(2,1)S(1)} %down_products.6.refs_3_), channel_id=1, source_target_pairs={{0,4},{4,0},{1,5},{5,1},{2,6},{6,2},{3,7},{7,3},{8,12},{12,8},{9,1... | collective-permute-start | bytes 2211848 | tf_op jit(solution)/shard_map/ppermute | solution.py:244
  189.0 34.5 %collective-permute-start.9 = (bf16[288,1280]{1,0:T(8,128)(2,1)S(1)}, bf16[288,1280]{1,0:T(8,128)(2,1)S(1)}, u32[]{:S(2)}, u32[]{:S(2)}) collective-permute-start(bf16[288,1280]{1,0:T(8,128)(2,1)S(1)} %down_products.5.refs_3_), channel_id=1, source_target_pairs={{0,4},{4,0},{1,5},{5,1},{2,6},{6,2},{3,7},{7,3},{8,12},{12,8},{9,1... | collective-permute-start | bytes 2211848 | tf_op jit(solution)/shard_map/ppermute | solution.py:244
  206.1 33.2 %collective-permute-start.14 = (bf16[288,1280]{1,0:T(8,128)(2,1)S(1)}, bf16[288,1280]{1,0:T(8,128)(2,1)S(1)}, u32[]{:S(2)}, u32[]{:S(2)}) collective-permute-start(bf16[288,1280]{1,0:T(8,128)(2,1)S(1)} %get-tuple-element.31.refs_3_), channel_id=1, source_target_pairs={{0,4},{4,0},{1,5},{5,1},{2,6},{6,2},{3,7},{7,3},{8,12},{12,8},{9,1... | collective-permute-start | bytes 2211848 | tf_op jit(solution)/shard_map/ppermute | solution.py:244
  207.1 48.1 %collective-permute-start.10 = (bf16[288,1280]{1,0:T(8,128)(2,1)S(1)}, bf16[288,1280]{1,0:T(8,128)(2,1)S(1)}, u32[]{:S(2)}, u32[]{:S(2)}) collective-permute-start(bf16[288,1280]{1,0:T(8,128)(2,1)S(1)} %get-tuple-element.34), channel_id=1, source_target_pairs={{0,4},{4,0},{1,5},{5,1},{2,6},{6,2},{3,7},{7,3},{8,12},{12,8},{9,1... | collective-permute-start | bytes 2211848 | tf_op jit(solution)/shard_map/ppermute | solution.py:244
  223.7 31.4 %collective-permute-start.13 = (bf16[288,1280]{1,0:T(8,128)(2,1)}, bf16[288,1280]{1,0:T(8,128)(2,1)}, u32[]{:S(2)}, u32[]{:S(2)}) collective-permute-start(bf16[288,1280]{1,0:T(8,128)(2,1)} %add_convert_fusion.2), channel_id=1, source_target_pairs={{0,1},{1,2},{2,3},{3,0},{4,5},{5,6},{6,7},{7,4},{8,9},{9,10},{10,1... | collective-permute-start | bytes 2211848 | tf_op jit(solution)/shard_map/ppermute | solution.py:265
  240.4 18.2 %collective-permute-start.15 = (bf16[288,1280]{1,0:T(8,128)(2,1)}, bf16[288,1280]{1,0:T(8,128)(2,1)}, u32[]{:S(2)}, u32[]{:S(2)}) collective-permute-start(bf16[288,1280]{1,0:T(8,128)(2,1)} %add_convert_fusion.1), channel_id=1, source_target_pairs={{0,3},{1,0},{2,1},{3,2},{4,7},{5,4},{6,5},{7,6},{8,11},{9,8},{10,9... | collective-permute-start | bytes 2211848 | tf_op jit(solution)/shard_map/ppermute | solution.py:265
  241.4 44.2 %collective-permute-start.11 = (bf16[288,1280]{1,0:T(8,128)(2,1)S(1)}, bf16[288,1280]{1,0:T(8,128)(2,1)}, u32[]{:S(2)}, u32[]{:S(2)}) collective-permute-start(bf16[288,1280]{1,0:T(8,128)(2,1)S(1)} %add_convert_fusion.3.refs_4_), channel_id=1, source_target_pairs={{0,2},{1,3},{2,0},{3,1},{4,6},{5,7},{6,4},{7,5},{8,10},{9,11},{10,... | collective-permute-start | bytes 2211848 | tf_op jit(solution)/shard_map/ppermute | solution.py:265
  241.4 46.3 %collective-permute-start.6 = (bf16[224,1280]{1,0:T(8,128)(2,1)}, bf16[224,1280]{1,0:T(8,128)(2,1)S(1)}, u32[]{:S(2)}, u32[]{:S(2)}) collective-permute-start(bf16[224,1280]{1,0:T(8,128)(2,1)} %bitcast.29), channel_id=1, source_target_pairs={{0,4},{4,0},{1,5},{5,1},{2,6},{6,2},{3,7},{7,3},{8,12},{12,8},{9,1... | collective-permute-start | bytes 1720328 | tf_op jit(solution)/shard_map/ppermute | solution.py:254
Sparse Core Ops, SparseCore 0:
  8.9 52.6 all-gather.2
  63.2 58.8 all-gather.4
  124.4 45.7 reduce-scatter.4
  172.5 46.4 reduce-scatter.2

commit v2 on v1

--- a/solution.py
+++ b/solution.py
@@ -9,18 +9,21 @@
 
 D = 10240
 CHUNKS = (7, 9)
+MICROSECOND = 10**6
 
 
 def order_of(line):
+    last = line - 1
     return (
         [("norm", 0), ("upo", 0, 0), ("upo", 0, 1), ("upw", 0), ("gelu", 0, 0), ("gelu", 0, 1)]
-        + [("s", 0, "o"), ("s", 0, "w"), ("norm", 1), ("upo", 1, 0), ("upo", 1, 1)]
+        + [("s", 0), ("norm", 1), ("upo", 1, 0), ("upo", 1, 1)]
         + [("upw", 1), ("gelu", 1, 0), ("gelu", 1, 1)]
         + [("do", 1, 0, 1), ("do", 1, 1, 1), ("do", 1, 2, line - 2)]
-        + [("dw", 1, 0, line // 2), ("m", 1, 0)]
-        + [("dw", 1, line // 2, line - line // 2)]
-        + [("m", 1, k) for k in range(1, line - 1)]
-        + [("x", 0), ("sum", 0), ("fin", 1)]
+        + [("dw", 1, 0, 2), ("m", 1, 0), ("dw", 1, 2, 1, 20 * MICROSECOND)]
+        + [("m", 1, 1), ("dw", 1, 3, line - 3)]
+        + [("m", 1, k) for k in range(2, last)]
+        + [("x", 0), ("acc", 1, 0, 0, 60 * MICROSECOND, ("x", 0), ("z", 1, 1))]
+        + [("sum", 0), ("fin", 1)]
     )
 
 
@@ -56,6 +59,48 @@
     )(side, normed, weights, *after)
 
 
+def gelu_kernel(own_ref, other_ref, *refs):
+    total = own_ref[...] + other_ref[...].astype(jnp.float32)
+    refs[-1][...] = (total * (0.5 + 0.5 * lax.erf(total * 0.5**0.5))).astype(jnp.bfloat16)
+
+
+def gelu_sum(own, other, first, tile, after):
+    rows, width = other.shape
+    return pl.pallas_call(
+        gelu_kernel,
+        grid=(width // tile,),
+        in_specs=[
+            pl.BlockSpec((rows, tile), lambda j: (0, first + j)),
+            pl.BlockSpec((rows, tile), lambda j: (0, j)),
+        ]
+        + [pl.BlockSpec(memory_space=pl.ANY)] * len(after),
+        out_specs=pl.BlockSpec((rows, tile), lambda j: (0, j)),
+        out_shape=jax.ShapeDtypeStruct((rows, width), jnp.bfloat16),
+        compiler_params=pltpu.CompilerParams(vmem_limit_bytes=40 * 2**20),
+        cost_estimate=pl.CostEstimate(flops=1000, bytes_accessed=1000, transcendentals=0),
+        name="gelu_sum",
+    )(own, other, *after)
+
+
+def add_kernel(left_ref, right_ref, *refs):
+    refs[-1][...] = left_ref[...].astype(jnp.float32) + right_ref[...].astype(jnp.float32)
+
+
+def add_pieces(left, right, after, weight):
+    rows, width = left.shape
+    return pl.pallas_call(
+        add_kernel,
+        grid=(1,),
+        in_specs=[pl.BlockSpec((rows, width), lambda j: (0, 0))] * 2
+        + [pl.BlockSpec(memory_space=pl.ANY)] * len(after),
+        out_specs=pl.BlockSpec((rows, width), lambda j: (0, 0)),
+        out_shape=jax.ShapeDtypeStruct((rows, width), jnp.float32),
+        compiler_params=pltpu.CompilerParams(vmem_limit_bytes=40 * 2**20),
+        cost_estimate=pl.CostEstimate(flops=1000 * weight, bytes_accessed=1000, transcendentals=0),
+        name="add_pieces",
+    )(left, right, *after)
+
+
 def down_kernel(parts, waits, blocks_ref, *refs):
     lefts, right_ref, outs = refs[:parts], refs[parts], refs[parts + 1 + waits :]
     total, begin = None, 0
@@ -73,7 +118,7 @@
             out[...] = total.astype(out.dtype)
 
 
-def down_products(hidden, weights, table, first, count, columns, after=()):
+def down_products(hidden, weights, table, first, count, columns, after=(), weight=1):
     rows = hidden[0].shape[0]
     if columns % 128:
         whole = jnp.concatenate(hidden, axis=1)
@@ -101,7 +146,7 @@
         ),
         out_shape=[jax.ShapeDtypeStruct((rows, columns), jnp.bfloat16)] * count,
         compiler_params=pltpu.CompilerParams(vmem_limit_bytes=40 * 2**20),
-        cost_estimate=pl.CostEstimate(flops=1000, bytes_accessed=1000, transcendentals=0),
+        cost_estimate=pl.CostEstimate(flops=1000 * weight, bytes_accessed=1000, transcendentals=0),
         name="down_products",
     )(table, *hidden, weights, *after)
 
@@ -119,26 +164,33 @@
     out_ref[0] = total.astype(out_ref.dtype)
 
 
-def stacked_products(hidden, weights, side, line, columns, after):
+def stacked_products(hidden, weights, sides, line, columns, after):
     rows = hidden[0].shape[0]
     if columns % 128:
-        table = side[0] * line + jnp.arange(line, dtype=jnp.int32)
-        return jnp.stack(down_products(hidden, weights, table, 0, line, columns))
+        both = []
+        for s in range(2):
+            table = sides[s] * line + jnp.arange(line, dtype=jnp.int32)
+            both.append(jnp.stack(down_products(hidden, weights, table, 0, line, columns)))
+        return jnp.concatenate(both, axis=2)
     return pl.pallas_call(
         functools.partial(stacked_kernel, len(hidden)),
         grid_spec=pltpu.PrefetchScalarGridSpec(
             num_scalar_prefetch=1,
-            grid=(line,),
-            in_specs=[pl.BlockSpec(piece.shape, lambda p, side: (0, 0)) for piece in hidden]
-            + [pl.BlockSpec((weights.shape[0], columns), lambda p, side: (0, side[0] * line + p))]
+            grid=(line, 2),
+            in_specs=[pl.BlockSpec(piece.shape, lambda p, s, sides: (0, 0)) for piece in hidden]
+            + [
+                pl.BlockSpec(
+                    (weights.shape[0], columns), lambda p, s, sides: (0, sides[s] * line + p)
+                )
+            ]
             + [pl.BlockSpec(memory_space=pl.ANY)] * len(after),
-            out_specs=pl.BlockSpec((1, rows, columns), lambda p, side: (p, 0, 0)),
+            out_specs=pl.BlockSpec((1, rows, columns), lambda p, s, sides: (p, 0, s)),
         ),
-        out_shape=jax.ShapeDtypeStruct((line, rows, columns), jnp.bfloat16),
+        out_shape=jax.ShapeDtypeStruct((line, rows, 2 * columns), jnp.bfloat16),
         compiler_params=pltpu.CompilerParams(vmem_limit_bytes=40 * 2**20),
         cost_estimate=pl.CostEstimate(flops=1000, bytes_accessed=1000, transcendentals=0),
         name="stacked_products",
-    )(side, *hidden, weights, *after)
+    )(sides, *hidden, weights, *after)
 
 
 def normalize(values, totals, gain_row):
@@ -164,7 +216,7 @@
     row = (place + jnp.array(shifts, jnp.int32)) % line
     table = jnp.concatenate([(1 - half) * line + row, half * line + row])
     here = half.astype(jnp.int32).reshape(1)
-    picks = {"o": 1 - here, "w": here}
+    picks = {"o": 1 - here, "w": here, "wo": jnp.concatenate([here, 1 - here])}
     table, picks, mine = lax.optimization_barrier((table, picks, mine))
     mine = mine + lax.ppermute(mine, "con", swap)
     mine = jnp.concatenate([mine.reshape(1, 2 * rows), wide(gain).reshape(1, columns)], axis=1)
@@ -195,7 +247,7 @@
         last.append(f(*args))
         return last[-1]
 
-    def task(kind, c, k=0, count=0, *awaited):
+    def task(kind, c, k=0, count=0, weight=1, *awaited):
         last.extend(have[key] for key in awaited)
         a, b = spans[c]
         if kind == "norm":
@@ -221,21 +273,17 @@
                 weights,
             )
         elif kind == "gelu":
-            if k:
-                have["gelu", c, 0], have["upo", c, 1] = lax.optimization_barrier(
-                    (have["gelu", c, 0], have["upo", c, 1])
-                )
-            have[kind, c, k] = plain(
-                lambda x, y: jax.nn.gelu(
-                    x[:, split[k] * tile : split[k + 1] * tile] + wide(y), approximate=False
-                ).astype(jnp.bfloat16),
+            have["gelu", c, k] = run(
+                lambda x, y, after: gelu_sum(x, y, split[k], tile, after),
                 have["upw", c],
                 have["upo", c, k],
             )
         elif kind in ("do", "dw"):
             first = k + line * (kind == "dw")
             outs = run(
-                lambda h, v, after: down_products(h, v, table, first, count, columns, after),
+                lambda h, v, after: down_products(
+                    h, v, table, first, count, columns, after, weight
+                ),
                 [have["gelu", c, 0], have["gelu", c, 1]],
                 down_weight,
             )
@@ -245,16 +293,18 @@
                 )
         elif kind == "s":
             out = run(
-                lambda h, v, after: stacked_products(h, v, picks[k], line, columns, after),
+                lambda h, v, after: stacked_products(h, v, picks["wo"], line, columns, after),
                 [have["gelu", c, 0], have["gelu", c, 1]],
                 down_weight,
             )
-            have["s" + k, c] = lax.psum_scatter(out, "out", scatter_dimension=0)
+            have[kind, c] = lax.psum_scatter(out, "out", scatter_dimension=0)
         elif kind == "x":
-            have[kind, c] = lax.ppermute(have["so", c], "con", swap)
+            have[kind, c] = lax.ppermute(have["s", c][:, columns:], "con", swap)
         elif kind == "sum":
             have["fin", c] = plain(
-                lambda x, y: (wide(x) + wide(y)).astype(jnp.bfloat16), have["sw", c], have["x", c]
+                lambda x, y: (wide(x[:, :columns]) + wide(y)).astype(jnp.bfloat16),
+                have["s", c],
+                have["x", c],
             )
         elif kind == "m":
             out = plain(
@@ -265,12 +315,18 @@
             have["z", c, k] = lax.ppermute(
                 out, "out", [(p, (p + shifts[k]) % line) for p in range(line)]
             )
+        elif kind == "acc":
+            have[kind, c] = run(
+                lambda x, y, after: add_pieces(x, y, after, weight),
+                have["pw", c, line - 1],
+                have["z", c, 0],
+            )
         else:
             have[kind, c] = plain(
                 lambda *terms: sum(wide(term) for term in terms).astype(jnp.bfloat16),
-                have["pw", c, line - 1],
+                have["acc", c],
                 have["po", c, line - 1],
-                *[have["z", c, i] for i in range(line - 1)],
+                *[have["z", c, i] for i in range(1, line - 1)],
             )
 
     for word in order_of(line):

time: 297 us -> 278 us (0.936)
  waiting for transfers between devices: 85.2 us -> 67.4 us
  other arithmetic: 25.8 us -> 10.7 us
  starting transfers between devices: 19 us -> 24 us
  local copies, waits for them, and re-layouts: 40.3 us -> 44.7 us
  Pallas kernels: 113 us -> 117 us
    ppermute x4, waiting for transfers between devices: 35.6 us -> 6.43 us  [task(): lax.ppermute(out, 'con', swap)]
    convert_element_type x4 -> x1, other arithmetic: 12.7 us -> 0.14 us  [task(): (wide(x[:, :columns]) + wide(y)).astype(jnp.bfloat16)]
    ppermute x3, waiting for transfers between devices: 30.4 us -> 36.5 us  [task(): lax.ppermute(out, 'out', [(p, (p + shifts[k]) % line) for p in range(line)])]
    ppermute x4, waiting for transfers between devices: 13 us -> 18.6 us  [task(): have[kind, c, k] = lax.ppermute(out, 'con', swap)]
    ppermute x3, starting transfers between devices: 1.04 us -> 5.23 us  [task(): lax.ppermute(out, 'out', [(p, (p + shifts[k]) % line) for p in range(line)])]
    pallas_call x5 -> x6, Pallas kernels: 34.9 us -> 38.8 us  [down_products(): pl.pallas_call(functools.partial(down_kernel, len(hidden), len(after)), g...]
    pallas_call x0 -> x5, Pallas kernels: none -> 3.56 us  [the longest x4 2.25 us: gelu_sum(): pl.pallas_call(gelu_kernel, grid=(width // tile,), in_specs=[pl.BlockSpec...]
    pallas_call x2 -> x1, Pallas kernels: 23.8 us -> 21.5 us  [stacked_products(): pl.pallas_call(functools.partial(stacked_kernel, len(hidden)), grid_spec=...]
  transfers between devices with their start and end apart: 20 -> 19, of which waited for: 11 -> 11; matrix products, arithmetic and copies ran while one was open for 20% -> 17% of each run, Pallas kernels for 38% -> 42%
where the time goes in v2:
time: 278 us; the launch traced here: 277 us
  Pallas kernels  117 us (42%)
  waiting for transfers between devices  67.4 us (24%)
  local copies, waits for them, and re-layouts  44.7 us (16%)
  starting transfers between devices  24 us (9%)
  between operations  13.5 us (5%)
  other arithmetic  10.7 us (4%)
    pallas_call x6, Pallas kernels, up_product(): pl.pallas_call(up_kernel, grid_spec=pltpu.PrefetchScalarGridSpec(num_scal...  53 us
    unnamed x23, local copies, waits for them, and re-layouts  39.4 us
    pallas_call x6, Pallas kernels, down_products(): pl.pallas_call(functools.partial(down_kernel, len(hidden), len(after)), g...  38.8 us
    ppermute x3, waiting for transfers between devices, task(): lax.ppermute(out, 'out', [(p, (p + shifts[k]) % line) for p in range(line)])  36.5 us
    pallas_call x1, Pallas kernels, stacked_products(): pl.pallas_call(functools.partial(stacked_kernel, len(hidden)), grid_spec=...  21.5 us
    ppermute x4, waiting for transfers between devices, task(): have[kind, c, k] = lax.ppermute(out, 'con', swap)  18.6 us
    ppermute x4, waiting for transfers between devices, task(): lax.ppermute(out, 'con', swap)  6.43 us
    ppermute x3, starting transfers between devices, local(): lax.ppermute(mine, 'out', [(p, (p + s) % line) for p in range(line)])  5.79 us
  transfers between devices with their start and end apart: 19, of which 11 were waited for; matrix products, arithmetic and copies ran while one was open for 17% of the time, Pallas kernels for 42%

profile of v2, /device:TPU:0, one launch (start us, length us, event | category | flops | bytes accessed | tf_op | source)
XLA Modules:
  0.0 277.1 jit_solution(5224620379336611344)
XLA Ops:
  6.5 2.0 slice.42
  8.6 2.0 slice.51
  11.4 3.0 %collective-permute-start = (f32[2,512]{1,0:T(2,128)S(1)}, f32[2,512]{1,0:T(2,128)S(1)}, u32[]{:S(2)}, u32[]{:S(2)}) collective-permute-start(f32[2,512]{1,0:T(2,128)S(1)} %pad_maximum_fusion.5), channel_id=1, source_target_pairs={{0,4},{4,0},{1,5},{5,1},{2,6},{6,2},{3,7},{7,3},{8,12},{12,8},{9,1... | collective-permute-start | bytes 12296 | tf_op jit(solution)/shard_map/ppermute | solution.py:221
  14.5 1.6 collective-permute-done
  16.1 4.2 %collective-permute-start.3 = (f32[1,2304]{1,0:T(1,128)S(1)}, f32[1,2304]{1,0:T(1,128)S(1)}, u32[]{:S(2)}, u32[]{:S(2)}) collective-permute-start(f32[1,2304]{1,0:T(1,128)S(1)} %constant_dynamic-update-slice_fusion), channel_id=1, source_target_pairs={{0,3},{1,0},{2,1},{3,2},{4,7},{5,4},{6,5},{7,6},{8,11},{9,8},{10,9... | collective-permute-start | bytes 27656 | tf_op jit(solution)/shard_map/ppermute | solution.py:224
  20.2 35.2 %copy.9 = bf16[5120,2,2560]{2,0,1:T(8,128)(2,1)} copy(bf16[5120,2,2560]{2,1,0:T(2,128)(2,1)} %param.7) | data formatting | bytes 104857600 | tf_op args[2]
  55.6 1.5 collective-permute-start.1
  57.2 3.3 %collective-permute-done.2 = f32[1,2304]{1,0:T(1,128)S(1)} collective-permute-done((f32[1,2304]{1,0:T(1,128)S(1)}, f32[1,2304]{1,0:T(1,128)S(1)}, u32[]{:S(2)}, u32[]{:S(2)}) %collective-permute-start.2) | collective-permute-done | bytes 9248 | tf_op jit(solution)/shard_map/ppermute | solution.py:224
  60.5 0.8 collective-permute-done.1
  61.6 2.5 multiply_convert_fusion.1.left_ref.refs_1_
  64.1 8.3 %up_product.6.refs_0_ = bf16[224,1536]{1,0:T(8,128)(2,1)S(1)} custom-call(s32[1]{0:T(128)S(6)} %sub.43.side_ref, bf16[224,5120]{1,0:T(8,128)(2,1)S(1)} %multiply_convert_fusion.1.left_ref.refs_1_, bf16[2,5120,2560]{2,1,0:T(8,128)(2,1)} %bitcast.12, bf16[2,5120,2560]{2,1,0:T(8,128)(2,1)} %bitcast.13, bf16[224,5120]{1,0:T(8,128)(2,1)S(1)} %multiply_convert_fusion.1.left_ref.refs_1_), custom_call_target="tpu_custom_call" | custom-call | flops 1000 | bytes 1000 | tf_op jit(solution)/shard_map/up_product/pallas_call | solution.py:43
  72.5 1.6 collective-permute-start.4
  74.1 5.5 %up_product.7.refs_0_ = bf16[224,1024]{1,0:T(8,128)(2,1)S(1)} custom-call(s32[1]{0:T(128)S(6)} %sub.43.side_ref, bf16[224,5120]{1,0:T(8,128)(2,1)S(1)} %multiply_convert_fusion.1.left_ref.refs_1_, bf16[2,5120,2560]{2,1,0:T(8,128)(2,1)} %bitcast.14, bf16[224,1536]{1,0:T(8,128)(2,1)S(1)} %up_product.6.refs_0_), custom_call_target="tpu_custom_call" | custom-call | flops 1000 | bytes 1000 | tf_op jit(solution)/shard_map/up_product/pallas_call | solution.py:43
  80.1 11.8 %up_product.8.own_ref.refs_0_ = f32[224,2560]{1,0:T(8,128)S(1)} custom-call(s32[1]{0:T(128)} %bitcast.side_ref, bf16[224,5120]{1,0:T(8,128)(2,1)S(1)} %multiply_convert_fusion.1.left_ref.refs_1_, bf16[2,5120,2560]{2,1,0:T(8,128)(2,1)} %bitcast.15, bf16[224,1024]{1,0:T(8,128)(2,1)S(1)} %up_product.7.refs_0_), custom_call_target="tpu_custom_call" | custom-call | flops 1000 | bytes 1000 | tf_op jit(solution)/shard_map/up_product/pallas_call | solution.py:43
  92.6 6.9 %collective-permute-done.5.other_ref = bf16[224,1024]{1,0:T(8,128)(2,1)S(1)} collective-permute-done((bf16[224,1024]{1,0:T(8,128)(2,1)S(1)}, bf16[224,1024]{1,0:T(8,128)(2,1)S(1)}, u32[]{:S(2)}, u32[]{:S(2)}) %collective-permute-start.5) | collective-permute-done | bytes 458784 | tf_op jit(solution)/shard_map/ppermute | solution.py:266
  99.9 21.5 %stacked_products.1.refs_0_ = bf16[4,224,2560]{2,1,0:T(8,128)(2,1)S(1)} custom-call(s32[2]{0:T(128)S(1)} %pad_add_fusion.1.side_ref, bf16[224,1536]{1,0:T(8,128)(2,1)S(1)} %gelu_sum.4.refs_0_, bf16[224,1024]{1,0:T(8,128)(2,1)S(1)} %gelu_sum.5.refs_1_.refs_3_, bf16[2560,10240]{1,0:T(8,128)(2,1)} %refs_2_.13, bf16[224,1024]{1,0:T(8,128)(2,1)S(1)} %gelu_sum.5.refs_1_.refs_3_), custom_call_target="tpu_custom_call" | custom-call | flops 1000 | bytes 1000 | tf_op jit(solution)/shard_map/stacked_products/pallas_call | solution.py:175
  121.4 2.1 copy-done
  123.6 3.2 %multiply_convert_fusion.left_ref.refs_1_ = bf16[288,5120]{1,0:T(8,128)(2,1)S(1)} fusion(bf16[288,5120]{1,0:T(8,128)(2,1)} %all-gather.5.cloned.1.call-done, f32[5120]{0:T(1024)S(1)} %pad_maximum_fusion.4, f32[288]{0:T(512)S(1)} %add_rsqrt_fusion, f32[288]{0:T(512)S(1)} %get-tuple-element.33), kind=kLoop, calls=%fused_computation.1 | loop fusion | flops 7372800 | bytes 5921024 | tf_op jit(solution)/shard_map/convert_element_type | solution.py:199
  126.8 8.7 %up_product.9.refs_0_ = bf16[288,1536]{1,0:T(8,128)(2,1)S(1)} custom-call(s32[1]{0:T(128)S(6)} %sub.43.side_ref, bf16[288,5120]{1,0:T(8,128)(2,1)S(1)} %multiply_convert_fusion.left_ref.refs_1_, bf16[2,5120,2560]{2,1,0:T(8,128)(2,1)} %bitcast.16, bf16[4,224,2560]{2,1,0:T(8,128)(2,1)S(1)} %copy-done.1, bf16[288,5120]{1,0:T(8,128)(2,1)S(1)} %multiply_convert_fusion.left_ref.refs_1_), custom_call_target="tpu_custom_call" | custom-call | flops 1000 | bytes 1000 | tf_op jit(solution)/shard_map/up_product/pallas_call | solution.py:43
  135.5 1.4 collective-permute-start.7
  136.9 5.9 %up_product.10.refs_0_ = bf16[288,1024]{1,0:T(8,128)(2,1)S(1)} custom-call(s32[1]{0:T(128)S(6)} %sub.43.side_ref, bf16[288,5120]{1,0:T(8,128)(2,1)S(1)} %multiply_convert_fusion.left_ref.refs_1_, bf16[2,5120,2560]{2,1,0:T(8,128)(2,1)} %bitcast.17, bf16[288,1536]{1,0:T(8,128)(2,1)S(1)} %up_product.9.refs_0_), custom_call_target="tpu_custom_call" | custom-call | flops 1000 | bytes 1000 | tf_op jit(solution)/shard_map/up_product/pallas_call | solution.py:43
  142.9 0.7 collective-permute-start.8
  143.6 12.8 %up_product.11.own_ref.refs_0_ = f32[288,2560]{1,0:T(8,128)S(1)} custom-call(s32[1]{0:T(128)} %bitcast.side_ref, bf16[288,5120]{1,0:T(8,128)(2,1)S(1)} %multiply_convert_fusion.left_ref.refs_1_, bf16[2,5120,2560]{2,1,0:T(8,128)(2,1)} %bitcast.18, bf16[288,1024]{1,0:T(8,128)(2,1)S(1)} %up_product.10.refs_0_), custom_call_target="tpu_custom_call" | custom-call | flops 1000 | bytes 1000 | tf_op jit(solution)/shard_map/up_product/pallas_call | solution.py:43
  156.4 1.8 collective-permute-done.7.other_ref
  158.2 0.7 gelu_sum.6.refs_0_
  158.9 9.8 %collective-permute-done.8.other_ref = bf16[288,1024]{1,0:T(8,128)(2,1)S(1)} collective-permute-done((bf16[288,1024]{1,0:T(8,128)(2,1)S(1)}, bf16[288,1024]{1,0:T(8,128)(2,1)S(1)}, u32[]{:S(2)}, u32[]{:S(2)}) %collective-permute-start.8) | collective-permute-done | bytes 589856 | tf_op jit(solution)/shard_map/ppermute | solution.py:266
  169.2 5.6 %down_products.6.refs_3_ = bf16[288,1280]{1,0:T(8,128)(2,1)S(1)} custom-call(s32[8]{0:T(128)S(1)} %pad_add_fusion.blocks_ref, bf16[288,1536]{1,0:T(8,128)(2,1)S(1)} %gelu_sum.6.refs_0_, bf16[288,1024]{1,0:T(8,128)(2,1)S(1)} %gelu_sum.7.refs_1_.refs_3_, bf16[2560,10240]{1,0:T(8,128)(2,1)} %refs_2_.13, bf16[288,1024]{1,0:T(8,128)(2,1)S(1)} %gelu_sum.7.refs_1_.refs_3_), custom_call_target="tpu_custom_call" | custom-call | flops 1000 | bytes 1000 | tf_op jit(solution)/shard_map/down_products/pallas_call | solution.py:133
  174.8 1.4 collective-permute-start.9
  176.2 5.6 %down_products.7.refs_3_ = bf16[288,1280]{1,0:T(8,128)(2,1)S(1)} custom-call(s32[8]{0:T(128)S(1)} %pad_add_fusion.blocks_ref, bf16[288,1536]{1,0:T(8,128)(2,1)S(1)} %gelu_sum.6.refs_0_, bf16[288,1024]{1,0:T(8,128)(2,1)S(1)} %gelu_sum.7.refs_1_.refs_3_, bf16[2560,10240]{1,0:T(8,128)(2,1)} %refs_2_.13, bf16[288,1280]{1,0:T(8,128)(2,1)S(1)} %down_products.6.refs_3_), custom_call_target="tpu_custom_call" | custom-call | flops 1000 | bytes 1000 | tf_op jit(solution)/shard_map/down_products/pallas_call | solution.py:133
  181.8 0.7 collective-permute-start.10
  182.5 8.8 %down_products.8 = (bf16[288,1280]{1,0:T(8,128)(2,1)}, bf16[288,1280]{1,0:T(8,128)(2,1)S(1)}) custom-call(s32[8]{0:T(128)S(1)} %pad_add_fusion.blocks_ref, bf16[288,1536]{1,0:T(8,128)(2,1)S(1)} %gelu_sum.6.refs_0_, bf16[288,1024]{1,0:T(8,128)(2,1)S(1)} %gelu_sum.7.refs_1_.refs_3_, bf16[2560,10240]{1,0:T(8,128)(2,1)} %refs_2_.13, ...), custom_call_target="tpu_custom_call" | custom-call | flops 1000 | bytes 1000 | tf_op jit(solution)/shard_map/down_products/pallas_call | solution.py:133
  191.3 0.9 copy-done.4
  192.1 1.5 collective-permute-start.12
  193.7 7.7 %down_products.9 = (bf16[288,1280]{1,0:T(8,128)(2,1)S(1)}, bf16[288,1280]{1,0:T(8,128)(2,1)S(1)}) custom-call(s32[8]{0:T(128)S(1)} %pad_add_fusion.blocks_ref, bf16[288,1536]{1,0:T(8,128)(2,1)S(1)} %gelu_sum.6.refs_0_, bf16[288,1024]{1,0:T(8,128)(2,1)S(1)} %gelu_sum.7.refs_1_.refs_3_, bf16[2560,10240]{1,0:T(8,128)(2,1)} %refs_2_.13, ...), custom_call_target="tpu_custom_call" | custom-call | flops 1000 | bytes 1000 | tf_op jit(solution)/shard_map/down_products/pallas_call | solution.py:133
  201.4 1.1 add_convert_fusion.3.refs_4_
  202.6 1.4 collective-permute-start.11
  204.0 6.2 %collective-permute-done.10 = bf16[288,1280]{1,0:T(8,128)(2,1)S(1)} collective-permute-done((bf16[288,1280]{1,0:T(8,128)(2,1)S(1)}, bf16[288,1280]{1,0:T(8,128)(2,1)S(1)}, u32[]{:S(2)}, u32[]{:S(2)}) %collective-permute-start.10) | collective-permute-done | bytes 737312 | tf_op jit(solution)/shard_map/ppermute | solution.py:292
  210.4 1.1 slice.58
  211.5 1.4 collective-permute-start.6
  212.9 1.1 copy-done.3
  214.0 5.6 %down_products.10.refs_3_ = bf16[288,1280]{1,0:T(8,128)(2,1)S(1)} custom-call(s32[8]{0:T(128)S(1)} %pad_add_fusion.blocks_ref, bf16[288,1536]{1,0:T(8,128)(2,1)S(1)} %gelu_sum.6.refs_0_, bf16[288,1024]{1,0:T(8,128)(2,1)S(1)} %gelu_sum.7.refs_1_.refs_3_, bf16[2560,10240]{1,0:T(8,128)(2,1)} %refs_2_.13, bf16[288,1280]{1,0:T(8,128)(2,1)S(1)} %copy-done.3, ...), custom_call_target="tpu_custom_call" | custom-call | flops 20000000000 | bytes 1000 | tf_op jit(solution)/shard_map/down_products/pallas_call | solution.py:133
  220.3 5.5 %down_products.11.left_ref.refs_0_ = bf16[288,1280]{1,0:T(8,128)(2,1)S(1)} custom-call(s32[8]{0:T(128)S(1)} %pad_add_fusion.blocks_ref, bf16[288,1536]{1,0:T(8,128)(2,1)S(1)} %gelu_sum.6.refs_0_, bf16[288,1024]{1,0:T(8,128)(2,1)S(1)} %gelu_sum.7.refs_1_.refs_3_, bf16[2560,10240]{1,0:T(8,128)(2,1)} %refs_2_.13, bf16[288,1280]{1,0:T(8,128)(2,1)S(1)} %down_products.10.refs_3_, ...), custom_call_target="tpu_custom_call" | custom-call | flops 1000 | bytes 1000 | tf_op jit(solution)/shard_map/down_products/pallas_call | solution.py:133
  226.0 1.3 add_convert_fusion.1.refs_1_
  227.4 3.8 %collective-permute-start.15 = (bf16[288,1280]{1,0:T(8,128)(2,1)S(1)}, bf16[288,1280]{1,0:T(8,128)(2,1)S(1)}, u32[]{:S(2)}, u32[]{:S(2)}) collective-permute-start(bf16[288,1280]{1,0:T(8,128)(2,1)S(1)} %add_convert_fusion.1.refs_1_), channel_id=1, source_target_pairs={{0,3},{1,0},{2,1},{3,2},{4,7},{5,4},{6,5},{7,6},{8,11},{9,8},{10,9... | collective-permute-start | bytes 2211848 | tf_op jit(solution)/shard_map/ppermute | solution.py:315
  231.2 22.8 %collective-permute-done.11.right_ref = bf16[288,1280]{1,0:T(8,128)(2,1)} collective-permute-done((bf16[288,1280]{1,0:T(8,128)(2,1)}, bf16[288,1280]{1,0:T(8,128)(2,1)}, u32[]{:S(2)}, u32[]{:S(2)}) %collective-permute-start.11) | collective-permute-done | bytes 737312 | tf_op jit(solution)/shard_map/ppermute | solution.py:315
  253.9 1.3 add_pieces.1
  255.4 13.7 %collective-permute-done.15 = bf16[288,1280]{1,0:T(8,128)(2,1)S(1)} collective-permute-done((bf16[288,1280]{1,0:T(8,128)(2,1)S(1)}, bf16[288,1280]{1,0:T(8,128)(2,1)S(1)}, u32[]{:S(2)}, u32[]{:S(2)}) %collective-permute-start.15) | collective-permute-done | bytes 737312 | tf_op jit(solution)/shard_map/ppermute | solution.py:315
  269.4 1.1 pad_maximum_fusion
  (68 shorter events, 5.2 us)
Async XLA Ops:
  6.5 4.2 %copy-start.9 = (s32[4]{0:T(128)S(1)}, s32[4]{0:T(128)}, u32[]{:S(2)}) copy-start(s32[4]{0:T(128)} %constant.79.clone) | copy-start | bytes 52
  6.5 4.4 %copy-start.6 = (bf16[512,1280]{1,0:T(8,128)(2,1)S(1)}, bf16[512,1280]{1,0:T(8,128)(2,1)}, u32[]{:S(2)}) copy-start(bf16[512,1280]{1,0:T(8,128)(2,1)} %param.5) | copy-start | bytes 3932164
  6.5 55.1 %all-gather.3.cloned.1.call-start = ((), (), s32[]{:S(2)}) async-start(), calls=%async_computation.1 | async-start | bytes 2867200 | tf_op jit(solution)/shard_map/all_gather | solution.py:211
  8.5 5.9 %copy-start.8 = (bf16[1280]{0:T(1024)(128)(2,1)S(1)}, bf16[1280]{0:T(1024)(128)(2,1)}, u32[]{:S(2)}) copy-start(bf16[1280]{0:T(1024)(128)(2,1)} %param.6) | copy-start | bytes 7684
  8.6 115.1 %all-gather.5.cloned.1.call-start = ((), (), s32[]{:S(2)}) async-start(), calls=%async_computation.3 | async-start | bytes 3686400 | tf_op jit(solution)/shard_map/all_gather | solution.py:211
  10.7 199.7 %reduce-scatter.2.cloned.1.call-start = ((), (), s32[]{:S(2)}) async-start(), calls=%async_computation.2 | async-start | bytes 5734400 | tf_op jit(solution)/shard_map/reduce_scatter | solution.py:300
  11.4 4.6 %collective-permute-start = (f32[2,512]{1,0:T(2,128)S(1)}, f32[2,512]{1,0:T(2,128)S(1)}, u32[]{:S(2)}, u32[]{:S(2)}) collective-permute-start(f32[2,512]{1,0:T(2,128)S(1)} %pad_maximum_fusion.5), channel_id=1, source_target_pairs={{0,4},{4,0},{1,5},{5,1},{2,6},{6,2},{3,7},{7,3},{8,12},{12,8},{9,1... | collective-permute-start | bytes 12296 | tf_op jit(solution)/shard_map/ppermute | solution.py:221
  16.1 41.0 %collective-permute-start.3 = (f32[1,2304]{1,0:T(1,128)S(1)}, f32[1,2304]{1,0:T(1,128)S(1)}, u32[]{:S(2)}, u32[]{:S(2)}) collective-permute-start(f32[1,2304]{1,0:T(1,128)S(1)} %constant_dynamic-update-slice_fusion), channel_id=1, source_target_pairs={{0,3},{1,0},{2,1},{3,2},{4,7},{5,4},{6,5},{7,6},{8,11},{9,8},{10,9... | collective-permute-start | bytes 27656 | tf_op jit(solution)/shard_map/ppermute | solution.py:224
  55.5 4.9 %collective-permute-start.2 = (f32[1,2304]{1,0:T(1,128)S(1)}, f32[1,2304]{1,0:T(1,128)S(1)}, u32[]{:S(2)}, u32[]{:S(2)}) collective-permute-start(f32[1,2304]{1,0:T(1,128)S(1)} %constant_dynamic-update-slice_fusion), channel_id=1, source_target_pairs={{0,2},{1,3},{2,0},{3,1},{4,6},{5,7},{6,4},{7,5},{8,10},{9,11},{10,... | collective-permute-start | bytes 27656 | tf_op jit(solution)/shard_map/ppermute | solution.py:224
  55.6 5.6 %collective-permute-start.1 = (f32[1,2304]{1,0:T(1,128)S(1)}, f32[1,2304]{1,0:T(1,128)S(1)}, u32[]{:S(2)}, u32[]{:S(2)}) collective-permute-start(f32[1,2304]{1,0:T(1,128)S(1)} %constant_dynamic-update-slice_fusion), channel_id=1, source_target_pairs={{0,1},{1,2},{2,3},{3,0},{4,5},{5,6},{6,7},{7,4},{8,9},{9,10},{10,1... | collective-permute-start | bytes 27656 | tf_op jit(solution)/shard_map/ppermute | solution.py:224
  72.5 19.5 %collective-permute-start.4 = (bf16[224,1536]{1,0:T(8,128)(2,1)S(1)}, bf16[224,1536]{1,0:T(8,128)(2,1)S(1)}, u32[]{:S(2)}, u32[]{:S(2)}) collective-permute-start(bf16[224,1536]{1,0:T(8,128)(2,1)S(1)} %up_product.6.refs_0_), channel_id=1, source_target_pairs={{0,4},{4,0},{1,5},{5,1},{2,6},{6,2},{3,7},{7,3},{8,12},{12,8},{9,1... | collective-permute-start | bytes 2064392 | tf_op jit(solution)/shard_map/ppermute | solution.py:266
  79.5 20.0 %collective-permute-start.5 = (bf16[224,1024]{1,0:T(8,128)(2,1)S(1)}, bf16[224,1024]{1,0:T(8,128)(2,1)S(1)}, u32[]{:S(2)}, u32[]{:S(2)}) collective-permute-start(bf16[224,1024]{1,0:T(8,128)(2,1)S(1)} %up_product.7.refs_0_), channel_id=1, source_target_pairs={{0,4},{4,0},{1,5},{5,1},{2,6},{6,2},{3,7},{7,3},{8,12},{12,8},{9,1... | collective-permute-start | bytes 1376264 | tf_op jit(solution)/shard_map/ppermute | solution.py:266
  121.4 2.1 copy-start
  123.6 3.2 %copy-start.1 = (bf16[4,224,2560]{2,1,0:T(8,128)(2,1)S(1)}, bf16[4,224,2560]{2,1,0:T(8,128)(2,1)}, u32[]{:S(2)}) copy-start(bf16[4,224,2560]{2,1,0:T(8,128)(2,1)} %copy-done) | copy-start | bytes 13762564
  135.5 22.7 %collective-permute-start.7 = (bf16[288,1536]{1,0:T(8,128)(2,1)S(1)}, bf16[288,1536]{1,0:T(8,128)(2,1)S(1)}, u32[]{:S(2)}, u32[]{:S(2)}) collective-permute-start(bf16[288,1536]{1,0:T(8,128)(2,1)S(1)} %up_product.9.refs_0_), channel_id=1, source_target_pairs={{0,4},{4,0},{1,5},{5,1},{2,6},{6,2},{3,7},{7,3},{8,12},{12,8},{9,1... | collective-permute-start | bytes 2654216 | tf_op jit(solution)/shard_map/ppermute | solution.py:266
  142.9 25.8 %collective-permute-start.8 = (bf16[288,1024]{1,0:T(8,128)(2,1)S(1)}, bf16[288,1024]{1,0:T(8,128)(2,1)S(1)}, u32[]{:S(2)}, u32[]{:S(2)}) collective-permute-start(bf16[288,1024]{1,0:T(8,128)(2,1)S(1)} %up_product.10.refs_0_), channel_id=1, source_target_pairs={{0,4},{4,0},{1,5},{5,1},{2,6},{6,2},{3,7},{7,3},{8,12},{12,8},{9,1... | collective-permute-start | bytes 1769480 | tf_op jit(solution)/shard_map/ppermute | solution.py:266
  174.8 26.6 %collective-permute-start.9 = (bf16[288,1280]{1,0:T(8,128)(2,1)S(1)}, bf16[288,1280]{1,0:T(8,128)(2,1)S(1)}, u32[]{:S(2)}, u32[]{:S(2)}) collective-permute-start(bf16[288,1280]{1,0:T(8,128)(2,1)S(1)} %down_products.6.refs_3_), channel_id=1, source_target_pairs={{0,4},{4,0},{1,5},{5,1},{2,6},{6,2},{3,7},{7,3},{8,12},{12,8},{9,1... | collective-permute-start | bytes 2211848 | tf_op jit(solution)/shard_map/ppermute | solution.py:292
  181.8 28.3 %collective-permute-start.10 = (bf16[288,1280]{1,0:T(8,128)(2,1)S(1)}, bf16[288,1280]{1,0:T(8,128)(2,1)S(1)}, u32[]{:S(2)}, u32[]{:S(2)}) collective-permute-start(bf16[288,1280]{1,0:T(8,128)(2,1)S(1)} %down_products.7.refs_3_), channel_id=1, source_target_pairs={{0,4},{4,0},{1,5},{5,1},{2,6},{6,2},{3,7},{7,3},{8,12},{12,8},{9,1... | collective-permute-start | bytes 2211848 | tf_op jit(solution)/shard_map/ppermute | solution.py:292
  191.3 0.9 copy-start.4
  192.1 33.9 %collective-permute-start.12 = (bf16[288,1280]{1,0:T(8,128)(2,1)}, bf16[288,1280]{1,0:T(8,128)(2,1)}, u32[]{:S(2)}, u32[]{:S(2)}) collective-permute-start(bf16[288,1280]{1,0:T(8,128)(2,1)} %get-tuple-element.23.refs_3_), channel_id=1, source_target_pairs={{0,4},{4,0},{1,5},{5,1},{2,6},{6,2},{3,7},{7,3},{8,12},{12,8},{9,1... | collective-permute-start | bytes 2211848 | tf_op jit(solution)/shard_map/ppermute | solution.py:292
  201.4 8.7 %copy-start.2 = (bf16[288,1280]{1,0:T(8,128)(2,1)}, bf16[288,1280]{1,0:T(8,128)(2,1)S(1)}, u32[]{:S(2)}) copy-start(bf16[288,1280]{1,0:T(8,128)(2,1)S(1)} %get-tuple-element.24.refs_3_) | copy-start | bytes 2211844
  202.6 51.3 %collective-permute-start.11 = (bf16[288,1280]{1,0:T(8,128)(2,1)}, bf16[288,1280]{1,0:T(8,128)(2,1)}, u32[]{:S(2)}, u32[]{:S(2)}) collective-permute-start(bf16[288,1280]{1,0:T(8,128)(2,1)} %add_convert_fusion.3.refs_4_), channel_id=1, source_target_pairs={{0,2},{1,3},{2,0},{3,1},{4,6},{5,7},{6,4},{7,5},{8,10},{9,11},{10,... | collective-permute-start | bytes 2211848 | tf_op jit(solution)/shard_map/ppermute | solution.py:315
  210.3 43.6 %collective-permute-start.13 = (bf16[288,1280]{1,0:T(8,128)(2,1)S(1)}, bf16[288,1280]{1,0:T(8,128)(2,1)S(1)}, u32[]{:S(2)}, u32[]{:S(2)}) collective-permute-start(bf16[288,1280]{1,0:T(8,128)(2,1)S(1)} %add_convert_fusion.2.refs_4_), channel_id=1, source_target_pairs={{0,1},{1,2},{2,3},{3,0},{4,5},{5,6},{6,7},{7,4},{8,9},{9,10},{10,1... | collective-permute-start | bytes 2211848 | tf_op jit(solution)/shard_map/ppermute | solution.py:315
  211.5 42.4 %collective-permute-start.6 = (bf16[224,1280]{1,0:T(8,128)(2,1)S(1)}, bf16[224,1280]{1,0:T(8,128)(2,1)S(1)}, u32[]{:S(2)}, u32[]{:S(2)}) collective-permute-start(bf16[224,1280]{1,0:T(8,128)(2,1)S(1)} %slice.58), channel_id=1, source_target_pairs={{0,4},{4,0},{1,5},{5,1},{2,6},{6,2},{3,7},{7,3},{8,12},{12,8},{9,1... | collective-permute-start | bytes 1720328 | tf_op jit(solution)/shard_map/ppermute | solution.py:302
  212.9 1.1 copy-start.3
  214.0 5.6 %copy-start.5 = (bf16[288,1280]{1,0:T(8,128)(2,1)S(1)}, bf16[288,1280]{1,0:T(8,128)(2,1)}, u32[]{:S(2)}) copy-start(bf16[288,1280]{1,0:T(8,128)(2,1)} %copy-done.4) | copy-start | bytes 2211844
  219.6 35.8 %collective-permute-start.14 = (bf16[288,1280]{1,0:T(8,128)(2,1)S(1)}, bf16[288,1280]{1,0:T(8,128)(2,1)S(1)}, u32[]{:S(2)}, u32[]{:S(2)}) collective-permute-start(bf16[288,1280]{1,0:T(8,128)(2,1)S(1)} %copy-done.5), channel_id=1, source_target_pairs={{0,4},{4,0},{1,5},{5,1},{2,6},{6,2},{3,7},{7,3},{8,12},{12,8},{9,1... | collective-permute-start | bytes 2211848 | tf_op jit(solution)/shard_map/ppermute | solution.py:292
  227.4 27.9 %copy-start.7 = (bf16[1,224,2560]{2,1,0:T(8,128)(2,1)S(1)}, bf16[1,224,2560]{2,1,0:T(8,128)(2,1)}, u32[]{:S(2)}) copy-start(bf16[1,224,2560]{2,1,0:T(8,128)(2,1)} %reduce-scatter.2.cloned.1.call-done) | copy-start | bytes 3440644
  227.4 41.8 %collective-permute-start.15 = (bf16[288,1280]{1,0:T(8,128)(2,1)S(1)}, bf16[288,1280]{1,0:T(8,128)(2,1)S(1)}, u32[]{:S(2)}, u32[]{:S(2)}) collective-permute-start(bf16[288,1280]{1,0:T(8,128)(2,1)S(1)} %add_convert_fusion.1.refs_1_), channel_id=1, source_target_pairs={{0,3},{1,0},{2,1},{3,2},{4,7},{5,4},{6,5},{7,6},{8,11},{9,8},{10,9... | collective-permute-start | bytes 2211848 | tf_op jit(solution)/shard_map/ppermute | solution.py:315
Sparse Core Ops, SparseCore 0:
  8.9 52.6 all-gather.2
  63.2 58.9 all-gather.4
  124.5 82.0 reduce-scatter.1

commit v3 on v2

--- a/solution.py
+++ b/solution.py
@@ -18,9 +18,8 @@
         [("norm", 0), ("upo", 0, 0), ("upo", 0, 1), ("upw", 0), ("gelu", 0, 0), ("gelu", 0, 1)]
         + [("s", 0), ("norm", 1), ("upo", 1, 0), ("upo", 1, 1)]
         + [("upw", 1), ("gelu", 1, 0), ("gelu", 1, 1)]
-        + [("do", 1, 0, 1), ("do", 1, 1, 1), ("do", 1, 2, line - 2)]
-        + [("dw", 1, 0, 2), ("m", 1, 0), ("dw", 1, 2, 1, 20 * MICROSECOND)]
-        + [("m", 1, 1), ("dw", 1, 3, line - 3)]
+        + [("do", 1, 0, 1), ("dw", 1, 0, 1), ("do", 1, 1, 1), ("do", 1, 2, line - 2), ("m", 1, 0)]
+        + [("dw", 1, 1, 1, 20 * MICROSECOND), ("m", 1, 1), ("dw", 1, 2, line - 2)]
         + [("m", 1, k) for k in range(2, last)]
         + [("x", 0), ("acc", 1, 0, 0, 60 * MICROSECOND, ("x", 0), ("z", 1, 1))]
         + [("sum", 0), ("fin", 1)]
@@ -212,8 +211,13 @@
 
     values = wide(tokens)
     mine = jnp.stack([jnp.sum(values, axis=1), jnp.sum(values * values, axis=1)])
-    shifts = sorted(range(line), key=lambda s: (-min(s, line - s), s))
-    row = (place + jnp.array(shifts, jnp.int32)) % line
+    four = line == 4
+    if four:
+        shifts = [3, 1, 2, 0]
+        row = jnp.stack([place ^ s for s in shifts])
+    else:
+        shifts = sorted(range(line), key=lambda s: (-min(s, line - s), s))
+        row = (place + jnp.array(shifts, jnp.int32)) % line
     table = jnp.concatenate([(1 - half) * line + row, half * line + row])
     here = half.astype(jnp.int32).reshape(1)
     picks = {"o": 1 - here, "w": here, "wo": jnp.concatenate([here, 1 - here])}
@@ -307,14 +311,18 @@
                 have["x", c],
             )
         elif kind == "m":
-            out = plain(
-                lambda x, y: (wide(x) + wide(y)).astype(jnp.bfloat16),
-                have["pw", c, k],
-                have["po", c, k],
-            )
-            have["z", c, k] = lax.ppermute(
-                out, "out", [(p, (p + shifts[k]) % line) for p in range(line)]
-            )
+            terms = [have["pw", c, k], have["po", c, k]]
+            if four and k == 2:
+                terms.append(have["ends", c])
+            out = plain(lambda *terms: sum(map(wide, terms)).astype(jnp.bfloat16), *terms)
+            if four and k == 0:
+                have["ends", c] = lax.ppermute(out, "out", [(0, 1), (3, 2)])
+                pairs = [(1, 2), (2, 1)]
+            elif four:
+                pairs = [(p, p ^ shifts[k]) for p in range(line)]
+            else:
+                pairs = [(p, (p + shifts[k]) % line) for p in range(line)]
+            have["z", c, k] = lax.ppermute(out, "out", pairs)
         elif kind == "acc":
             have[kind, c] = run(
                 lambda x, y, after: add_pieces(x, y, after, weight),

time: 278 us -> 269 us (0.968)
  waiting for transfers between devices: 67.4 us -> 57.6 us
    ppermute x3 -> x4, waiting for transfers between devices: 36.5 us -> 13 us  [the longest x3 13 us: task(): have['z', c, k] = lax.ppermute(out, 'out', pairs)]
    ppermute x4, waiting for transfers between devices: 6.43 us -> 18 us  [task(): lax.ppermute(out, 'con', swap)]
    unnamed x23 -> x17, local copies, waits for them, and re-layouts: 39.4 us -> 37.5 us
  transfers between devices with their start and end apart: 19 -> 20, of which waited for: 11 -> 12; matrix products, arithmetic and copies ran while one was open for 17% -> 18% of each run, Pallas kernels for 42% -> 44%
where the time goes in v3:
time: 269 us; the launch traced here: 268 us
  Pallas kernels  117 us (43%)
  waiting for transfers between devices  57.6 us (21%)
  local copies, waits for them, and re-layouts  42.7 us (16%)
  starting transfers between devices  25.1 us (9%)
  between operations  13.4 us (5%)
  other arithmetic  12.2 us (5%)
    pallas_call x6, Pallas kernels, up_product(): pl.pallas_call(up_kernel, grid_spec=pltpu.PrefetchScalarGridSpec(num_scal...  52.7 us
    pallas_call x6, Pallas kernels, down_products(): pl.pallas_call(functools.partial(down_kernel, len(hidden), len(after)), g...  38.6 us
    unnamed x17, local copies, waits for them, and re-layouts  37.5 us
    pallas_call x1, Pallas kernels, stacked_products(): pl.pallas_call(functools.partial(stacked_kernel, len(hidden)), grid_spec=...  21.5 us
    ppermute x4, waiting for transfers between devices, task(): have[kind, c, k] = lax.ppermute(out, 'con', swap)  18.6 us
    ppermute x4, waiting for transfers between devices, task(): lax.ppermute(out, 'con', swap)  18 us
    ppermute x3, waiting for transfers between devices, task(): have['z', c, k] = lax.ppermute(out, 'out', pairs)  13 us
    ppermute x3, starting transfers between devices, local(): lax.ppermute(mine, 'out', [(p, (p + s) % line) for p in range(line)])  5.73 us
  transfers between devices with their start and end apart: 20, of which 12 were waited for; matrix products, arithmetic and copies ran while one was open for 18% of the time, Pallas kernels for 44%

profile of v3, /device:TPU:0, one launch (start us, length us, event | category | flops | bytes accessed | tf_op | source)
XLA Modules:
  0.0 267.7 jit_solution(3079402313757348889)
XLA Ops:
  6.5 2.0 slice.42
  8.6 2.0 slice.51
  11.5 3.0 %collective-permute-start = (f32[2,512]{1,0:T(2,128)S(1)}, f32[2,512]{1,0:T(2,128)S(1)}, u32[]{:S(2)}, u32[]{:S(2)}) collective-permute-start(f32[2,512]{1,0:T(2,128)S(1)} %pad_maximum_fusion.5), channel_id=1, source_target_pairs={{0,4},{4,0},{1,5},{5,1},{2,6},{6,2},{3,7},{7,3},{8,12},{12,8},{9,1... | collective-permute-start | bytes 12296 | tf_op jit(solution)/shard_map/ppermute | solution.py:225
  14.5 1.6 collective-permute-done
  16.1 4.2 %collective-permute-start.3 = (f32[1,2304]{1,0:T(1,128)S(1)}, f32[1,2304]{1,0:T(1,128)S(1)}, u32[]{:S(2)}, u32[]{:S(2)}) collective-permute-start(f32[1,2304]{1,0:T(1,128)S(1)} %constant_dynamic-update-slice_fusion), channel_id=1, source_target_pairs={{0,3},{1,0},{2,1},{3,2},{4,7},{5,4},{6,5},{7,6},{8,11},{9,8},{10,9... | collective-permute-start | bytes 27656 | tf_op jit(solution)/shard_map/ppermute | solution.py:228
  20.3 35.3 %copy.8 = bf16[5120,2,2560]{2,0,1:T(8,128)(2,1)} copy(bf16[5120,2,2560]{2,1,0:T(2,128)(2,1)} %param.6) | data formatting | bytes 104857600 | tf_op args[2]
  55.6 1.5 collective-permute-start.1
  57.1 3.3 %collective-permute-done.2 = f32[1,2304]{1,0:T(1,128)S(1)} collective-permute-done((f32[1,2304]{1,0:T(1,128)S(1)}, f32[1,2304]{1,0:T(1,128)S(1)}, u32[]{:S(2)}, u32[]{:S(2)}) %collective-permute-start.2) | collective-permute-done | bytes 9248 | tf_op jit(solution)/shard_map/ppermute | solution.py:228
  61.6 2.5 multiply_convert_fusion.1.left_ref.refs_1_
  64.2 8.2 %up_product.6.refs_0_ = bf16[224,1536]{1,0:T(8,128)(2,1)S(1)} custom-call(s32[1]{0:T(128)S(6)} %sub.43.side_ref, bf16[224,5120]{1,0:T(8,128)(2,1)S(1)} %multiply_convert_fusion.1.left_ref.refs_1_, bf16[2,5120,2560]{2,1,0:T(8,128)(2,1)} %bitcast.16, bf16[2,5120,2560]{2,1,0:T(8,128)(2,1)} %bitcast.17, bf16[224,5120]{1,0:T(8,128)(2,1)S(1)} %multiply_convert_fusion.1.left_ref.refs_1_), custom_call_target="tpu_custom_call" | custom-call | flops 1000 | bytes 1000 | tf_op jit(solution)/shard_map/up_product/pallas_call | solution.py:42
  72.3 1.7 collective-permute-start.4
  74.0 5.5 %up_product.7.refs_0_ = bf16[224,1024]{1,0:T(8,128)(2,1)S(1)} custom-call(s32[1]{0:T(128)S(6)} %sub.43.side_ref, bf16[224,5120]{1,0:T(8,128)(2,1)S(1)} %multiply_convert_fusion.1.left_ref.refs_1_, bf16[2,5120,2560]{2,1,0:T(8,128)(2,1)} %bitcast.18, bf16[224,1536]{1,0:T(8,128)(2,1)S(1)} %up_product.6.refs_0_), custom_call_target="tpu_custom_call" | custom-call | flops 1000 | bytes 1000 | tf_op jit(solution)/shard_map/up_product/pallas_call | solution.py:42
  80.0 11.8 %up_product.8.own_ref.refs_0_ = f32[224,2560]{1,0:T(8,128)S(1)} custom-call(s32[1]{0:T(128)} %bitcast.4.side_ref, bf16[224,5120]{1,0:T(8,128)(2,1)S(1)} %multiply_convert_fusion.1.left_ref.refs_1_, bf16[2,5120,2560]{2,1,0:T(8,128)(2,1)} %bitcast.19, bf16[224,1024]{1,0:T(8,128)(2,1)S(1)} %up_product.7.refs_0_), custom_call_target="tpu_custom_call" | custom-call | flops 1000 | bytes 1000 | tf_op jit(solution)/shard_map/up_product/pallas_call | solution.py:42
  92.4 6.9 %collective-permute-done.5.other_ref = bf16[224,1024]{1,0:T(8,128)(2,1)S(1)} collective-permute-done((bf16[224,1024]{1,0:T(8,128)(2,1)S(1)}, bf16[224,1024]{1,0:T(8,128)(2,1)S(1)}, u32[]{:S(2)}, u32[]{:S(2)}) %collective-permute-start.5) | collective-permute-done | bytes 458784 | tf_op jit(solution)/shard_map/ppermute | solution.py:270
  99.7 21.5 %stacked_products.1.refs_0_ = bf16[4,224,2560]{2,1,0:T(8,128)(2,1)S(1)} custom-call(s32[2]{0:T(128)S(1)} %pad_add_fusion.2.side_ref, bf16[224,1536]{1,0:T(8,128)(2,1)S(1)} %gelu_sum.4.refs_0_, bf16[224,1024]{1,0:T(8,128)(2,1)S(1)} %gelu_sum.5.refs_1_.refs_3_, bf16[2560,10240]{1,0:T(8,128)(2,1)} %refs_2_.13, bf16[224,1024]{1,0:T(8,128)(2,1)S(1)} %gelu_sum.5.refs_1_.refs_3_), custom_call_target="tpu_custom_call" | custom-call | flops 1000 | bytes 1000 | tf_op jit(solution)/shard_map/stacked_products/pallas_call | solution.py:174
  121.2 2.1 copy-done
  123.4 3.2 %multiply_convert_fusion.left_ref.refs_1_ = bf16[288,5120]{1,0:T(8,128)(2,1)S(1)} fusion(bf16[288,5120]{1,0:T(8,128)(2,1)} %all-gather.5.cloned.1.call-done, f32[5120]{0:T(1024)S(1)} %pad_maximum_fusion.4, f32[288]{0:T(512)S(1)} %add_rsqrt_fusion, f32[288]{0:T(512)S(1)} %get-tuple-element.33), kind=kLoop, calls=%fused_computation.1 | loop fusion | flops 7372800 | bytes 5921024 | tf_op jit(solution)/shard_map/convert_element_type | solution.py:198
  126.6 8.6 %up_product.9.refs_0_ = bf16[288,1536]{1,0:T(8,128)(2,1)S(1)} custom-call(s32[1]{0:T(128)S(6)} %sub.43.side_ref, bf16[288,5120]{1,0:T(8,128)(2,1)S(1)} %multiply_convert_fusion.left_ref.refs_1_, bf16[2,5120,2560]{2,1,0:T(8,128)(2,1)} %bitcast.20, bf16[4,224,2560]{2,1,0:T(8,128)(2,1)S(1)} %copy-done.1, bf16[288,5120]{1,0:T(8,128)(2,1)S(1)} %multiply_convert_fusion.left_ref.refs_1_), custom_call_target="tpu_custom_call" | custom-call | flops 1000 | bytes 1000 | tf_op jit(solution)/shard_map/up_product/pallas_call | solution.py:42
  135.2 1.5 collective-permute-start.7
  136.7 5.9 %up_product.10.refs_0_ = bf16[288,1024]{1,0:T(8,128)(2,1)S(1)} custom-call(s32[1]{0:T(128)S(6)} %sub.43.side_ref, bf16[288,5120]{1,0:T(8,128)(2,1)S(1)} %multiply_convert_fusion.left_ref.refs_1_, bf16[2,5120,2560]{2,1,0:T(8,128)(2,1)} %bitcast.21, bf16[288,1536]{1,0:T(8,128)(2,1)S(1)} %up_product.9.refs_0_), custom_call_target="tpu_custom_call" | custom-call | flops 1000 | bytes 1000 | tf_op jit(solution)/shard_map/up_product/pallas_call | solution.py:42
  143.3 12.7 %up_product.11.own_ref.refs_0_ = f32[288,2560]{1,0:T(8,128)S(1)} custom-call(s32[1]{0:T(128)} %bitcast.4.side_ref, bf16[288,5120]{1,0:T(8,128)(2,1)S(1)} %multiply_convert_fusion.left_ref.refs_1_, bf16[2,5120,2560]{2,1,0:T(8,128)(2,1)} %bitcast.22, bf16[288,1024]{1,0:T(8,128)(2,1)S(1)} %up_product.10.refs_0_), custom_call_target="tpu_custom_call" | custom-call | flops 1000 | bytes 1000 | tf_op jit(solution)/shard_map/up_product/pallas_call | solution.py:42
  156.0 1.8 collective-permute-done.7.other_ref
  158.6 9.9 %collective-permute-done.8.other_ref = bf16[288,1024]{1,0:T(8,128)(2,1)S(1)} collective-permute-done((bf16[288,1024]{1,0:T(8,128)(2,1)S(1)}, bf16[288,1024]{1,0:T(8,128)(2,1)S(1)}, u32[]{:S(2)}, u32[]{:S(2)}) %collective-permute-start.8) | collective-permute-done | bytes 589856 | tf_op jit(solution)/shard_map/ppermute | solution.py:270
  169.2 5.5 %down_products.6.refs_3_ = bf16[288,1280]{1,0:T(8,128)(2,1)S(1)} custom-call(s32[8]{0:T(128)S(1)} %pad_add_fusion.1.blocks_ref, bf16[288,1536]{1,0:T(8,128)(2,1)S(1)} %gelu_sum.6.refs_0_, bf16[288,1024]{1,0:T(8,128)(2,1)S(1)} %gelu_sum.7.refs_1_.refs_3_, bf16[2560,10240]{1,0:T(8,128)(2,1)} %refs_2_.13, bf16[288,1024]{1,0:T(8,128)(2,1)S(1)} %gelu_sum.7.refs_1_.refs_3_), custom_call_target="tpu_custom_call" | custom-call | flops 1000 | bytes 1000 | tf_op jit(solution)/shard_map/down_products/pallas_call | solution.py:132
  174.7 1.7 collective-permute-start.9
  176.4 5.6 %down_products.7.refs_3_ = bf16[288,1280]{1,0:T(8,128)(2,1)S(1)} custom-call(s32[8]{0:T(128)S(1)} %pad_add_fusion.1.blocks_ref, bf16[288,1536]{1,0:T(8,128)(2,1)S(1)} %gelu_sum.6.refs_0_, bf16[288,1024]{1,0:T(8,128)(2,1)S(1)} %gelu_sum.7.refs_1_.refs_3_, bf16[2560,10240]{1,0:T(8,128)(2,1)} %refs_2_.13, bf16[288,1280]{1,0:T(8,128)(2,1)S(1)} %down_products.6.refs_3_), custom_call_target="tpu_custom_call" | custom-call | flops 1000 | bytes 1000 | tf_op jit(solution)/shard_map/down_products/pallas_call | solution.py:132
  182.0 5.6 %down_products.8.refs_3_ = bf16[288,1280]{1,0:T(8,128)(2,1)S(1)} custom-call(s32[8]{0:T(128)S(1)} %pad_add_fusion.1.blocks_ref, bf16[288,1536]{1,0:T(8,128)(2,1)S(1)} %gelu_sum.6.refs_0_, bf16[288,1024]{1,0:T(8,128)(2,1)S(1)} %gelu_sum.7.refs_1_.refs_3_, bf16[2560,10240]{1,0:T(8,128)(2,1)} %refs_2_.13, bf16[288,1280]{1,0:T(8,128)(2,1)S(1)} %down_products.7.refs_3_), custom_call_target="tpu_custom_call" | custom-call | flops 1000 | bytes 1000 | tf_op jit(solution)/shard_map/down_products/pallas_call | solution.py:132
  187.8 8.8 %down_products.9 = (bf16[288,1280]{1,0:T(8,128)(2,1)}, bf16[288,1280]{1,0:T(8,128)(2,1)S(1)}) custom-call(s32[8]{0:T(128)S(1)} %pad_add_fusion.1.blocks_ref, bf16[288,1536]{1,0:T(8,128)(2,1)S(1)} %gelu_sum.6.refs_0_, bf16[288,1024]{1,0:T(8,128)(2,1)S(1)} %gelu_sum.7.refs_1_.refs_3_, bf16[2560,10240]{1,0:T(8,128)(2,1)} %refs_2_.13, ...), custom_call_target="tpu_custom_call" | custom-call | flops 1000 | bytes 1000 | tf_op jit(solution)/shard_map/down_products/pallas_call | solution.py:132
  196.6 1.7 collective-permute-start.12
  198.2 1.0 add_convert_fusion.3.refs_4_
  199.3 2.2 collective-permute-start.13
  201.4 1.5 collective-permute-start.11
  203.0 5.5 %down_products.10.refs_3_ = bf16[288,1280]{1,0:T(8,128)(2,1)S(1)} custom-call(s32[8]{0:T(128)S(1)} %pad_add_fusion.1.blocks_ref, bf16[288,1536]{1,0:T(8,128)(2,1)S(1)} %gelu_sum.6.refs_0_, bf16[288,1024]{1,0:T(8,128)(2,1)S(1)} %gelu_sum.7.refs_1_.refs_3_, bf16[2560,10240]{1,0:T(8,128)(2,1)} %refs_2_.13, bf16[288,1280]{1,0:T(8,128)(2,1)} %get-tuple-element.23.refs_3_, ...), custom_call_target="tpu_custom_call" | custom-call | flops 20000000000 | bytes 1000 | tf_op jit(solution)/shard_map/down_products/pallas_call | solution.py:132
  208.4 1.6 collective-permute-done.10
  210.3 1.1 slice.58
  211.4 1.7 collective-permute-start.6
  213.0 7.7 %down_products.11 = (bf16[288,1280]{1,0:T(8,128)(2,1)S(1)}, bf16[288,1280]{1,0:T(8,128)(2,1)S(1)}) custom-call(s32[8]{0:T(128)S(1)} %pad_add_fusion.1.blocks_ref, bf16[288,1536]{1,0:T(8,128)(2,1)S(1)} %gelu_sum.6.refs_0_, bf16[288,1024]{1,0:T(8,128)(2,1)S(1)} %gelu_sum.7.refs_1_.refs_3_, bf16[2560,10240]{1,0:T(8,128)(2,1)} %refs_2_.13, ...), custom_call_target="tpu_custom_call" | custom-call | flops 1000 | bytes 1000 | tf_op jit(solution)/shard_map/down_products/pallas_call | solution.py:132
  220.8 5.1 %collective-permute-done.12 = bf16[288,1280]{1,0:T(8,128)(2,1)} collective-permute-done((bf16[288,1280]{1,0:T(8,128)(2,1)}, bf16[288,1280]{1,0:T(8,128)(2,1)}, u32[]{:S(2)}, u32[]{:S(2)}) %collective-permute-start.12) | collective-permute-done | bytes 737312 | tf_op jit(solution)/shard_map/ppermute | solution.py:296
  225.9 1.6 collective-permute-start.15
  227.5 1.7 add_convert_fusion.1.refs_1_
  229.2 1.3 collective-permute-start.16
  230.5 5.5 %collective-permute-done.14.refs_3_ = bf16[288,1280]{1,0:T(8,128)(2,1)} collective-permute-done((bf16[288,1280]{1,0:T(8,128)(2,1)S(1)}, bf16[288,1280]{1,0:T(8,128)(2,1)}, u32[]{:S(2)}, u32[]{:S(2)}) %collective-permute-start.14) | collective-permute-done | bytes 737312 | tf_op jit(solution)/shard_map/ppermute | solution.py:325
  236.0 2.1 collective-permute-done.6.refs_2_
  238.1 1.4 add_pieces.1
  239.7 11.3 %collective-permute-done.15 = bf16[288,1280]{1,0:T(8,128)(2,1)S(1)} collective-permute-done((bf16[288,1280]{1,0:T(8,128)(2,1)S(1)}, bf16[288,1280]{1,0:T(8,128)(2,1)S(1)}, u32[]{:S(2)}, u32[]{:S(2)}) %collective-permute-start.15) | collective-permute-done | bytes 737312 | tf_op jit(solution)/shard_map/ppermute | solution.py:296
  251.0 7.5 %collective-permute-done.16 = bf16[288,1280]{1,0:T(8,128)(2,1)S(1)} collective-permute-done((bf16[288,1280]{1,0:T(8,128)(2,1)S(1)}, bf16[288,1280]{1,0:T(8,128)(2,1)S(1)}, u32[]{:S(2)}, u32[]{:S(2)}) %collective-permute-start.16) | collective-permute-done | bytes 737312 | tf_op jit(solution)/shard_map/ppermute | solution.py:325
  258.5 1.5 add_convert_fusion
  260.0 1.1 pad_maximum_fusion
  (64 shorter events, 6.7 us)
Async XLA Ops:
  6.5 4.4 %copy-start.4 = (bf16[512,1280]{1,0:T(8,128)(2,1)S(1)}, bf16[512,1280]{1,0:T(8,128)(2,1)}, u32[]{:S(2)}) copy-start(bf16[512,1280]{1,0:T(8,128)(2,1)} %param.4) | copy-start | bytes 3932164
  6.5 55.1 %all-gather.3.cloned.1.call-start = ((), (), s32[]{:S(2)}) async-start(), calls=%async_computation.1 | async-start | bytes 2867200 | tf_op jit(solution)/shard_map/all_gather | solution.py:210
  8.5 6.0 %copy-start.6 = (bf16[1280]{0:T(1024)(128)(2,1)S(1)}, bf16[1280]{0:T(1024)(128)(2,1)}, u32[]{:S(2)}) copy-start(bf16[1280]{0:T(1024)(128)(2,1)} %param.5) | copy-start | bytes 7684
  8.6 114.9 %all-gather.5.cloned.1.call-start = ((), (), s32[]{:S(2)}) async-start(), calls=%async_computation.3 | async-start | bytes 3686400 | tf_op jit(solution)/shard_map/all_gather | solution.py:210
  10.7 199.6 %reduce-scatter.2.cloned.1.call-start = ((), (), s32[]{:S(2)}) async-start(), calls=%async_computation.2 | async-start | bytes 5734400 | tf_op jit(solution)/shard_map/reduce_scatter | solution.py:304
  11.5 4.6 %collective-permute-start = (f32[2,512]{1,0:T(2,128)S(1)}, f32[2,512]{1,0:T(2,128)S(1)}, u32[]{:S(2)}, u32[]{:S(2)}) collective-permute-start(f32[2,512]{1,0:T(2,128)S(1)} %pad_maximum_fusion.5), channel_id=1, source_target_pairs={{0,4},{4,0},{1,5},{5,1},{2,6},{6,2},{3,7},{7,3},{8,12},{12,8},{9,1... | collective-permute-start | bytes 12296 | tf_op jit(solution)/shard_map/ppermute | solution.py:225
  16.1 41.0 %collective-permute-start.3 = (f32[1,2304]{1,0:T(1,128)S(1)}, f32[1,2304]{1,0:T(1,128)S(1)}, u32[]{:S(2)}, u32[]{:S(2)}) collective-permute-start(f32[1,2304]{1,0:T(1,128)S(1)} %constant_dynamic-update-slice_fusion), channel_id=1, source_target_pairs={{0,3},{1,0},{2,1},{3,2},{4,7},{5,4},{6,5},{7,6},{8,11},{9,8},{10,9... | collective-permute-start | bytes 27656 | tf_op jit(solution)/shard_map/ppermute | solution.py:228
  55.5 4.9 %collective-permute-start.2 = (f32[1,2304]{1,0:T(1,128)S(1)}, f32[1,2304]{1,0:T(1,128)S(1)}, u32[]{:S(2)}, u32[]{:S(2)}) collective-permute-start(f32[1,2304]{1,0:T(1,128)S(1)} %constant_dynamic-update-slice_fusion), channel_id=1, source_target_pairs={{0,2},{1,3},{2,0},{3,1},{4,6},{5,7},{6,4},{7,5},{8,10},{9,11},{10,... | collective-permute-start | bytes 27656 | tf_op jit(solution)/shard_map/ppermute | solution.py:228
  55.6 5.8 %collective-permute-start.1 = (f32[1,2304]{1,0:T(1,128)S(1)}, f32[1,2304]{1,0:T(1,128)S(1)}, u32[]{:S(2)}, u32[]{:S(2)}) collective-permute-start(f32[1,2304]{1,0:T(1,128)S(1)} %constant_dynamic-update-slice_fusion), channel_id=1, source_target_pairs={{0,1},{1,2},{2,3},{3,0},{4,5},{5,6},{6,7},{7,4},{8,9},{9,10},{10,1... | collective-permute-start | bytes 27656 | tf_op jit(solution)/shard_map/ppermute | solution.py:228
  72.3 19.5 %collective-permute-start.4 = (bf16[224,1536]{1,0:T(8,128)(2,1)S(1)}, bf16[224,1536]{1,0:T(8,128)(2,1)S(1)}, u32[]{:S(2)}, u32[]{:S(2)}) collective-permute-start(bf16[224,1536]{1,0:T(8,128)(2,1)S(1)} %up_product.6.refs_0_), channel_id=1, source_target_pairs={{0,4},{4,0},{1,5},{5,1},{2,6},{6,2},{3,7},{7,3},{8,12},{12,8},{9,1... | collective-permute-start | bytes 2064392 | tf_op jit(solution)/shard_map/ppermute | solution.py:270
  79.5 19.8 %collective-permute-start.5 = (bf16[224,1024]{1,0:T(8,128)(2,1)S(1)}, bf16[224,1024]{1,0:T(8,128)(2,1)S(1)}, u32[]{:S(2)}, u32[]{:S(2)}) collective-permute-start(bf16[224,1024]{1,0:T(8,128)(2,1)S(1)} %up_product.7.refs_0_), channel_id=1, source_target_pairs={{0,4},{4,0},{1,5},{5,1},{2,6},{6,2},{3,7},{7,3},{8,12},{12,8},{9,1... | collective-permute-start | bytes 1376264 | tf_op jit(solution)/shard_map/ppermute | solution.py:270
  121.2 2.1 copy-start
  123.4 3.2 %copy-start.1 = (bf16[4,224,2560]{2,1,0:T(8,128)(2,1)S(1)}, bf16[4,224,2560]{2,1,0:T(8,128)(2,1)}, u32[]{:S(2)}) copy-start(bf16[4,224,2560]{2,1,0:T(8,128)(2,1)} %copy-done) | copy-start | bytes 13762564
  135.2 22.7 %collective-permute-start.7 = (bf16[288,1536]{1,0:T(8,128)(2,1)S(1)}, bf16[288,1536]{1,0:T(8,128)(2,1)S(1)}, u32[]{:S(2)}, u32[]{:S(2)}) collective-permute-start(bf16[288,1536]{1,0:T(8,128)(2,1)S(1)} %up_product.9.refs_0_), channel_id=1, source_target_pairs={{0,4},{4,0},{1,5},{5,1},{2,6},{6,2},{3,7},{7,3},{8,12},{12,8},{9,1... | collective-permute-start | bytes 2654216 | tf_op jit(solution)/shard_map/ppermute | solution.py:270
  142.6 25.8 %collective-permute-start.8 = (bf16[288,1024]{1,0:T(8,128)(2,1)S(1)}, bf16[288,1024]{1,0:T(8,128)(2,1)S(1)}, u32[]{:S(2)}, u32[]{:S(2)}) collective-permute-start(bf16[288,1024]{1,0:T(8,128)(2,1)S(1)} %up_product.10.refs_0_), channel_id=1, source_target_pairs={{0,4},{4,0},{1,5},{5,1},{2,6},{6,2},{3,7},{7,3},{8,12},{12,8},{9,1... | collective-permute-start | bytes 1769480 | tf_op jit(solution)/shard_map/ppermute | solution.py:270
  174.7 23.5 %collective-permute-start.9 = (bf16[288,1280]{1,0:T(8,128)(2,1)S(1)}, bf16[288,1280]{1,0:T(8,128)(2,1)S(1)}, u32[]{:S(2)}, u32[]{:S(2)}) collective-permute-start(bf16[288,1280]{1,0:T(8,128)(2,1)S(1)} %down_products.6.refs_3_), channel_id=1, source_target_pairs={{0,4},{4,0},{1,5},{5,1},{2,6},{6,2},{3,7},{7,3},{8,12},{12,8},{9,1... | collective-permute-start | bytes 2211848 | tf_op jit(solution)/shard_map/ppermute | solution.py:296
  187.5 22.5 %collective-permute-start.10 = (bf16[288,1280]{1,0:T(8,128)(2,1)S(1)}, bf16[288,1280]{1,0:T(8,128)(2,1)S(1)}, u32[]{:S(2)}, u32[]{:S(2)}) collective-permute-start(bf16[288,1280]{1,0:T(8,128)(2,1)S(1)} %down_products.8.refs_3_), channel_id=1, source_target_pairs={{0,4},{4,0},{1,5},{5,1},{2,6},{6,2},{3,7},{7,3},{8,12},{12,8},{9,1... | collective-permute-start | bytes 2211848 | tf_op jit(solution)/shard_map/ppermute | solution.py:296
  196.6 4.9 %copy-start.2 = (bf16[288,1280]{1,0:T(8,128)(2,1)}, bf16[288,1280]{1,0:T(8,128)(2,1)S(1)}, u32[]{:S(2)}) copy-start(bf16[288,1280]{1,0:T(8,128)(2,1)S(1)} %get-tuple-element.26) | copy-start | bytes 2211844
  196.6 29.3 %collective-permute-start.12 = (bf16[288,1280]{1,0:T(8,128)(2,1)}, bf16[288,1280]{1,0:T(8,128)(2,1)}, u32[]{:S(2)}, u32[]{:S(2)}) collective-permute-start(bf16[288,1280]{1,0:T(8,128)(2,1)} %get-tuple-element.23.refs_3_), channel_id=1, source_target_pairs={{0,4},{4,0},{1,5},{5,1},{2,6},{6,2},{3,7},{7,3},{8,12},{12,8},{9,1... | collective-permute-start | bytes 2211848 | tf_op jit(solution)/shard_map/ppermute | solution.py:296
  199.3 28.2 %collective-permute-start.13 = (bf16[288,1280]{1,0:T(8,128)(2,1)}, bf16[288,1280]{1,0:T(8,128)(2,1)}, u32[]{:S(2)}, u32[]{:S(2)}) collective-permute-start(bf16[288,1280]{1,0:T(8,128)(2,1)} %add_convert_fusion.3.refs_4_), channel_id=1, source_target_pairs={{0,1},{3,2},{4,5},{7,6},{8,9},{11,10},{12,13},{15,14},{16,17},{19,... | collective-permute-start | bytes 2211848 | tf_op jit(solution)/shard_map/ppermute | solution.py:319
  201.4 29.0 %collective-permute-start.11 = (bf16[288,1280]{1,0:T(8,128)(2,1)}, bf16[288,1280]{1,0:T(8,128)(2,1)}, u32[]{:S(2)}, u32[]{:S(2)}) collective-permute-start(bf16[288,1280]{1,0:T(8,128)(2,1)} %add_convert_fusion.3.refs_4_), channel_id=1, source_target_pairs={{1,2},{2,1},{5,6},{6,5},{9,10},{10,9},{13,14},{14,13},{17,18},{18,... | collective-permute-start | bytes 2211848 | tf_op jit(solution)/shard_map/ppermute | solution.py:325
  210.2 25.8 %collective-permute-start.14 = (bf16[288,1280]{1,0:T(8,128)(2,1)S(1)}, bf16[288,1280]{1,0:T(8,128)(2,1)}, u32[]{:S(2)}, u32[]{:S(2)}) collective-permute-start(bf16[288,1280]{1,0:T(8,128)(2,1)S(1)} %add_convert_fusion.2.refs_4_), channel_id=1, source_target_pairs={{0,1},{1,0},{2,3},{3,2},{4,5},{5,4},{6,7},{7,6},{8,9},{9,8},{10,11... | collective-permute-start | bytes 2211848 | tf_op jit(solution)/shard_map/ppermute | solution.py:325
  211.4 14.5 %copy-start.3 = (bf16[288,1280]{1,0:T(8,128)(2,1)S(1)}, bf16[288,1280]{1,0:T(8,128)(2,1)}, u32[]{:S(2)}) copy-start(bf16[288,1280]{1,0:T(8,128)(2,1)} %copy-done.2) | copy-start | bytes 2211844
  211.4 26.7 %collective-permute-start.6 = (bf16[224,1280]{1,0:T(8,128)(2,1)S(1)}, bf16[224,1280]{1,0:T(8,128)(2,1)S(1)}, u32[]{:S(2)}, u32[]{:S(2)}) collective-permute-start(bf16[224,1280]{1,0:T(8,128)(2,1)S(1)} %slice.58), channel_id=1, source_target_pairs={{0,4},{4,0},{1,5},{5,1},{2,6},{6,2},{3,7},{7,3},{8,12},{12,8},{9,1... | collective-permute-start | bytes 1720328 | tf_op jit(solution)/shard_map/ppermute | solution.py:306
  225.9 25.1 %collective-permute-start.15 = (bf16[288,1280]{1,0:T(8,128)(2,1)S(1)}, bf16[288,1280]{1,0:T(8,128)(2,1)S(1)}, u32[]{:S(2)}, u32[]{:S(2)}) collective-permute-start(bf16[288,1280]{1,0:T(8,128)(2,1)S(1)} %copy-done.3), channel_id=1, source_target_pairs={{0,4},{4,0},{1,5},{5,1},{2,6},{6,2},{3,7},{7,3},{8,12},{12,8},{9,1... | collective-permute-start | bytes 2211848 | tf_op jit(solution)/shard_map/ppermute | solution.py:296
  229.2 29.4 %collective-permute-start.16 = (bf16[288,1280]{1,0:T(8,128)(2,1)S(1)}, bf16[288,1280]{1,0:T(8,128)(2,1)S(1)}, u32[]{:S(2)}, u32[]{:S(2)}) collective-permute-start(bf16[288,1280]{1,0:T(8,128)(2,1)S(1)} %add_convert_fusion.1.refs_1_), channel_id=1, source_target_pairs={{0,2},{1,3},{2,0},{3,1},{4,6},{5,7},{6,4},{7,5},{8,10},{9,11},{10,... | collective-permute-start | bytes 2211848 | tf_op jit(solution)/shard_map/ppermute | solution.py:325
  238.1 1.5 copy-start.5
Sparse Core Ops, SparseCore 0:
  8.9 52.5 all-gather.2
  63.1 59.1 all-gather.4
  124.6 83.6 reduce-scatter.1

commit v4 on v3

--- a/solution.py
+++ b/solution.py
@@ -98,6 +98,27 @@
         cost_estimate=pl.CostEstimate(flops=1000 * weight, bytes_accessed=1000, transcendentals=0),
         name="add_pieces",
     )(left, right, *after)
+
+
+def finish_kernel(first_ref, *refs):
+    terms, out_ref = refs[:-1], refs[-1]
+    rows = first_ref.shape[0]
+    out_ref[:rows, :] = first_ref[...]
+    total = terms[0][...]
+    for term in terms[1:]:
+        total = total + term[...].astype(jnp.float32)
+    out_ref[rows:, :] = total.astype(out_ref.dtype)
+
+
+def finish(first, *terms):
+    rows = first.shape[0] + terms[0].shape[0]
+    return pl.pallas_call(
+        finish_kernel,
+        out_shape=jax.ShapeDtypeStruct((rows, first.shape[1]), jnp.bfloat16),
+        compiler_params=pltpu.CompilerParams(vmem_limit_bytes=40 * 2**20),
+        cost_estimate=pl.CostEstimate(flops=1000, bytes_accessed=1000, transcendentals=0),
+        name="finish",
+    )(first, *terms)
 
 
 def down_kernel(parts, waits, blocks_ref, *refs):
@@ -315,6 +336,8 @@
             if four and k == 2:
                 terms.append(have["ends", c])
             out = plain(lambda *terms: sum(map(wide, terms)).astype(jnp.bfloat16), *terms)
+            if k == line - 2:
+                out, have["s", 0] = lax.optimization_barrier((out, have["s", 0]))
             if four and k == 0:
                 have["ends", c] = lax.ppermute(out, "out", [(0, 1), (3, 2)])
                 pairs = [(1, 2), (2, 1)]
@@ -330,8 +353,8 @@
                 have["z", c, 0],
             )
         else:
-            have[kind, c] = plain(
-                lambda *terms: sum(wide(term) for term in terms).astype(jnp.bfloat16),
+            have[kind, c] = finish(
+                have["fin", 0],
                 have["acc", c],
                 have["po", c, line - 1],
                 *[have["z", c, i] for i in range(1, line - 1)],
@@ -339,7 +362,7 @@
 
     for word in order_of(line):
         task(*word)
-    return jnp.concatenate([have["fin", c] for c in range(len(spans))], axis=0)
+    return have["fin", 1]
 
 
 def solution(mesh):

time: 269 us -> 268 us (level)
  other arithmetic: 12.2 us -> 8.21 us
  local copies, waits for them, and re-layouts: 42.7 us -> 45.8 us
    ppermute x3, waiting for transfers between devices: 13 us -> 22.1 us  [task(): have['z', c, k] = lax.ppermute(out, 'out', pairs)]
    ppermute x4, waiting for transfers between devices: 18 us -> 9.83 us  [task(): lax.ppermute(out, 'con', swap)]
    unnamed x17 -> x21, local copies, waits for them, and re-layouts: 37.5 us -> 40.5 us
    ppermute x3, starting transfers between devices: 2.9 us -> 5.92 us  [task(): have['z', c, k] = lax.ppermute(out, 'out', pairs)]
  transfers between devices with their start and end apart: 20 -> 20, of which waited for: 12 -> 11; matrix products, arithmetic and copies ran while one was open for 18% -> 17% of each run, Pallas kernels for 44% -> 43%
where the time goes in v4:
time: 268 us; the launch traced here: 267 us
  Pallas kernels  117 us (44%)
  waiting for transfers between devices  56.4 us (21%)
  local copies, waits for them, and re-layouts  45.8 us (17%)
  starting transfers between devices  26.3 us (10%)
  between operations  13.5 us (5%)
  other arithmetic  8.21 us (3%)
    pallas_call x6, Pallas kernels, up_product(): pl.pallas_call(up_kernel, grid_spec=pltpu.PrefetchScalarGridSpec(num_scal...  52.7 us
    unnamed x21, local copies, waits for them, and re-layouts  40.5 us
    pallas_call x6, Pallas kernels, down_products(): pl.pallas_call(functools.partial(down_kernel, len(hidden), len(after)), g...  37.8 us
    ppermute x3, waiting for transfers between devices, task(): have['z', c, k] = lax.ppermute(out, 'out', pairs)  22.1 us
    pallas_call x1, Pallas kernels, stacked_products(): pl.pallas_call(functools.partial(stacked_kernel, len(hidden)), grid_spec=...  21.5 us
    ppermute x4, waiting for transfers between devices, task(): have[kind, c, k] = lax.ppermute(out, 'con', swap)  18.6 us
    ppermute x4, waiting for transfers between devices, task(): lax.ppermute(out, 'con', swap)  9.83 us
    ppermute x3, starting transfers between devices, task(): have['z', c, k] = lax.ppermute(out, 'out', pairs)  5.92 us
  transfers between devices with their start and end apart: 20, of which 11 were waited for; matrix products, arithmetic and copies ran while one was open for 17% of the time, Pallas kernels for 43%

profile of v4, /device:TPU:0, one launch (start us, length us, event | category | flops | bytes accessed | tf_op | source)
XLA Modules:
  0.0 267.4 jit_solution(11902439105933183869)
XLA Ops:
  6.5 2.0 slice.49
  8.6 2.0 slice.42
  11.5 3.0 %collective-permute-start = (f32[2,512]{1,0:T(2,128)S(1)}, f32[2,512]{1,0:T(2,128)S(1)}, u32[]{:S(2)}, u32[]{:S(2)}) collective-permute-start(f32[2,512]{1,0:T(2,128)S(1)} %pad_maximum_fusion.4), channel_id=1, source_target_pairs={{0,4},{4,0},{1,5},{5,1},{2,6},{6,2},{3,7},{7,3},{8,12},{12,8},{9,1... | collective-permute-start | bytes 12296 | tf_op jit(solution)/shard_map/ppermute | solution.py:246
  14.5 1.6 collective-permute-done
  16.1 4.2 %collective-permute-start.3 = (f32[1,2304]{1,0:T(1,128)S(1)}, f32[1,2304]{1,0:T(1,128)S(1)}, u32[]{:S(2)}, u32[]{:S(2)}) collective-permute-start(f32[1,2304]{1,0:T(1,128)S(1)} %constant_dynamic-update-slice_fusion), channel_id=1, source_target_pairs={{0,3},{1,0},{2,1},{3,2},{4,7},{5,4},{6,5},{7,6},{8,11},{9,8},{10,9... | collective-permute-start | bytes 27656 | tf_op jit(solution)/shard_map/ppermute | solution.py:249
  20.3 35.2 %copy.8 = bf16[5120,2,2560]{2,0,1:T(8,128)(2,1)} copy(bf16[5120,2,2560]{2,1,0:T(2,128)(2,1)} %param.6) | data formatting | bytes 104857600 | tf_op args[2]
  55.7 1.5 collective-permute-start.1
  57.2 3.2 %collective-permute-done.2 = f32[1,2304]{1,0:T(1,128)S(1)} collective-permute-done((f32[1,2304]{1,0:T(1,128)S(1)}, f32[1,2304]{1,0:T(1,128)S(1)}, u32[]{:S(2)}, u32[]{:S(2)}) %collective-permute-start.2) | collective-permute-done | bytes 9248 | tf_op jit(solution)/shard_map/ppermute | solution.py:249
  60.5 0.9 collective-permute-done.1
  61.6 2.5 multiply_convert_fusion.1.left_ref.refs_1_
  64.1 8.2 %up_product.6.refs_0_ = bf16[224,1536]{1,0:T(8,128)(2,1)S(1)} custom-call(s32[1]{0:T(128)S(6)} %sub.43.side_ref, bf16[224,5120]{1,0:T(8,128)(2,1)S(1)} %multiply_convert_fusion.1.left_ref.refs_1_, bf16[2,5120,2560]{2,1,0:T(8,128)(2,1)} %bitcast.16, bf16[2,5120,2560]{2,1,0:T(8,128)(2,1)} %bitcast.17, bf16[224,5120]{1,0:T(8,128)(2,1)S(1)} %multiply_convert_fusion.1.left_ref.refs_1_), custom_call_target="tpu_custom_call" | custom-call | flops 1000 | bytes 1000 | tf_op jit(solution)/shard_map/up_product/pallas_call | solution.py:42
  72.3 1.7 collective-permute-start.4
  74.0 5.5 %up_product.7.refs_0_ = bf16[224,1024]{1,0:T(8,128)(2,1)S(1)} custom-call(s32[1]{0:T(128)S(6)} %sub.43.side_ref, bf16[224,5120]{1,0:T(8,128)(2,1)S(1)} %multiply_convert_fusion.1.left_ref.refs_1_, bf16[2,5120,2560]{2,1,0:T(8,128)(2,1)} %bitcast.18, bf16[224,1536]{1,0:T(8,128)(2,1)S(1)} %up_product.6.refs_0_), custom_call_target="tpu_custom_call" | custom-call | flops 1000 | bytes 1000 | tf_op jit(solution)/shard_map/up_product/pallas_call | solution.py:42
  79.9 11.8 %up_product.8.own_ref.refs_0_ = f32[224,2560]{1,0:T(8,128)S(1)} custom-call(s32[1]{0:T(128)} %bitcast.4.side_ref, bf16[224,5120]{1,0:T(8,128)(2,1)S(1)} %multiply_convert_fusion.1.left_ref.refs_1_, bf16[2,5120,2560]{2,1,0:T(8,128)(2,1)} %bitcast.19, bf16[224,1024]{1,0:T(8,128)(2,1)S(1)} %up_product.7.refs_0_), custom_call_target="tpu_custom_call" | custom-call | flops 1000 | bytes 1000 | tf_op jit(solution)/shard_map/up_product/pallas_call | solution.py:42
  92.4 6.9 %collective-permute-done.5.other_ref = bf16[224,1024]{1,0:T(8,128)(2,1)S(1)} collective-permute-done((bf16[224,1024]{1,0:T(8,128)(2,1)S(1)}, bf16[224,1024]{1,0:T(8,128)(2,1)S(1)}, u32[]{:S(2)}, u32[]{:S(2)}) %collective-permute-start.5) | collective-permute-done | bytes 458784 | tf_op jit(solution)/shard_map/ppermute | solution.py:291
  99.7 21.5 %stacked_products.1.refs_0_ = bf16[4,224,2560]{2,1,0:T(8,128)(2,1)S(1)} custom-call(s32[2]{0:T(128)S(1)} %pad_add_fusion.2.side_ref, bf16[224,1536]{1,0:T(8,128)(2,1)S(1)} %gelu_sum.4.refs_0_, bf16[224,1024]{1,0:T(8,128)(2,1)S(1)} %gelu_sum.5.refs_1_.refs_3_, bf16[2560,10240]{1,0:T(8,128)(2,1)} %refs_2_.13, bf16[224,1024]{1,0:T(8,128)(2,1)S(1)} %gelu_sum.5.refs_1_.refs_3_), custom_call_target="tpu_custom_call" | custom-call | flops 1000 | bytes 1000 | tf_op jit(solution)/shard_map/stacked_products/pallas_call | solution.py:195
  121.2 2.1 copy-done
  123.4 3.2 %multiply_convert_fusion.left_ref.refs_1_ = bf16[288,5120]{1,0:T(8,128)(2,1)S(1)} fusion(bf16[288,5120]{1,0:T(8,128)(2,1)} %all-gather.3.cloned.1.call-done, f32[5120]{0:T(1024)S(1)} %pad_maximum_fusion.3, f32[288]{0:T(512)S(1)} %add_rsqrt_fusion, f32[288]{0:T(512)S(1)} %get-tuple-element.37), kind=kLoop, calls=%fused_computation.1 | loop fusion | flops 7372800 | bytes 5921024 | tf_op jit(solution)/shard_map/convert_element_type | solution.py:219
  126.6 8.6 %up_product.9.refs_0_ = bf16[288,1536]{1,0:T(8,128)(2,1)S(1)} custom-call(s32[1]{0:T(128)S(6)} %sub.43.side_ref, bf16[288,5120]{1,0:T(8,128)(2,1)S(1)} %multiply_convert_fusion.left_ref.refs_1_, bf16[2,5120,2560]{2,1,0:T(8,128)(2,1)} %bitcast.20, bf16[4,224,2560]{2,1,0:T(8,128)(2,1)S(1)} %copy-done.1, bf16[288,5120]{1,0:T(8,128)(2,1)S(1)} %multiply_convert_fusion.left_ref.refs_1_), custom_call_target="tpu_custom_call" | custom-call | flops 1000 | bytes 1000 | tf_op jit(solution)/shard_map/up_product/pallas_call | solution.py:42
  135.2 1.5 collective-permute-start.6
  136.7 5.9 %up_product.10.refs_0_ = bf16[288,1024]{1,0:T(8,128)(2,1)S(1)} custom-call(s32[1]{0:T(128)S(6)} %sub.43.side_ref, bf16[288,5120]{1,0:T(8,128)(2,1)S(1)} %multiply_convert_fusion.left_ref.refs_1_, bf16[2,5120,2560]{2,1,0:T(8,128)(2,1)} %bitcast.21, bf16[288,1536]{1,0:T(8,128)(2,1)S(1)} %up_product.9.refs_0_), custom_call_target="tpu_custom_call" | custom-call | flops 1000 | bytes 1000 | tf_op jit(solution)/shard_map/up_product/pallas_call | solution.py:42
  143.3 12.7 %up_product.11.own_ref.refs_0_ = f32[288,2560]{1,0:T(8,128)S(1)} custom-call(s32[1]{0:T(128)} %bitcast.4.side_ref, bf16[288,5120]{1,0:T(8,128)(2,1)S(1)} %multiply_convert_fusion.left_ref.refs_1_, bf16[2,5120,2560]{2,1,0:T(8,128)(2,1)} %bitcast.22, bf16[288,1024]{1,0:T(8,128)(2,1)S(1)} %up_product.10.refs_0_), custom_call_target="tpu_custom_call" | custom-call | flops 1000 | bytes 1000 | tf_op jit(solution)/shard_map/up_product/pallas_call | solution.py:42
  156.0 1.8 collective-permute-done.6.other_ref
  158.6 9.9 %collective-permute-done.7.other_ref = bf16[288,1024]{1,0:T(8,128)(2,1)S(1)} collective-permute-done((bf16[288,1024]{1,0:T(8,128)(2,1)S(1)}, bf16[288,1024]{1,0:T(8,128)(2,1)S(1)}, u32[]{:S(2)}, u32[]{:S(2)}) %collective-permute-start.7) | collective-permute-done | bytes 589856 | tf_op jit(solution)/shard_map/ppermute | solution.py:291
  169.2 5.5 %down_products.6.refs_3_ = bf16[288,1280]{1,0:T(8,128)(2,1)S(1)} custom-call(s32[8]{0:T(128)S(1)} %pad_add_fusion.1.blocks_ref, bf16[288,1536]{1,0:T(8,128)(2,1)S(1)} %gelu_sum.6.refs_0_, bf16[288,1024]{1,0:T(8,128)(2,1)S(1)} %gelu_sum.7.refs_1_.refs_3_, bf16[2560,10240]{1,0:T(8,128)(2,1)} %refs_2_.13, bf16[288,1024]{1,0:T(8,128)(2,1)S(1)} %gelu_sum.7.refs_1_.refs_3_), custom_call_target="tpu_custom_call" | custom-call | flops 1000 | bytes 1000 | tf_op jit(solution)/shard_map/down_products/pallas_call | solution.py:153
  174.7 1.7 collective-permute-start.8
  176.4 5.6 %down_products.7.refs_3_ = bf16[288,1280]{1,0:T(8,128)(2,1)S(1)} custom-call(s32[8]{0:T(128)S(1)} %pad_add_fusion.1.blocks_ref, bf16[288,1536]{1,0:T(8,128)(2,1)S(1)} %gelu_sum.6.refs_0_, bf16[288,1024]{1,0:T(8,128)(2,1)S(1)} %gelu_sum.7.refs_1_.refs_3_, bf16[2560,10240]{1,0:T(8,128)(2,1)} %refs_2_.13, bf16[288,1280]{1,0:T(8,128)(2,1)S(1)} %down_products.6.refs_3_), custom_call_target="tpu_custom_call" | custom-call | flops 1000 | bytes 1000 | tf_op jit(solution)/shard_map/down_products/pallas_call | solution.py:153
  182.0 5.6 %down_products.8.refs_3_ = bf16[288,1280]{1,0:T(8,128)(2,1)S(1)} custom-call(s32[8]{0:T(128)S(1)} %pad_add_fusion.1.blocks_ref, bf16[288,1536]{1,0:T(8,128)(2,1)S(1)} %gelu_sum.6.refs_0_, bf16[288,1024]{1,0:T(8,128)(2,1)S(1)} %gelu_sum.7.refs_1_.refs_3_, bf16[2560,10240]{1,0:T(8,128)(2,1)} %refs_2_.13, bf16[288,1280]{1,0:T(8,128)(2,1)S(1)} %down_products.7.refs_3_), custom_call_target="tpu_custom_call" | custom-call | flops 1000 | bytes 1000 | tf_op jit(solution)/shard_map/down_products/pallas_call | solution.py:153
  187.8 7.9 %down_products.9 = (bf16[288,1280]{1,0:T(8,128)(2,1)S(1)}, bf16[288,1280]{1,0:T(8,128)(2,1)S(1)}) custom-call(s32[8]{0:T(128)S(1)} %pad_add_fusion.1.blocks_ref, bf16[288,1536]{1,0:T(8,128)(2,1)S(1)} %gelu_sum.6.refs_0_, bf16[288,1024]{1,0:T(8,128)(2,1)S(1)} %gelu_sum.7.refs_1_.refs_3_, bf16[2560,10240]{1,0:T(8,128)(2,1)} %refs_2_.13, ...), custom_call_target="tpu_custom_call" | custom-call | flops 1000 | bytes 1000 | tf_op jit(solution)/shard_map/down_products/pallas_call | solution.py:153
  195.7 1.8 collective-permute-start.10
  197.6 1.3 collective-permute-start.11
  199.0 5.6 %down_products.10.refs_3_ = bf16[288,1280]{1,0:T(8,128)(2,1)S(1)} custom-call(s32[8]{0:T(128)S(1)} %pad_add_fusion.1.blocks_ref, bf16[288,1536]{1,0:T(8,128)(2,1)S(1)} %gelu_sum.6.refs_0_, bf16[288,1024]{1,0:T(8,128)(2,1)S(1)} %gelu_sum.7.refs_1_.refs_3_, bf16[2560,10240]{1,0:T(8,128)(2,1)} %refs_2_.13, bf16[288,1280]{1,0:T(8,128)(2,1)S(1)} %get-tuple-element.25.refs_3_, ...), custom_call_target="tpu_custom_call" | custom-call | flops 20000000000 | bytes 1000 | tf_op jit(solution)/shard_map/down_products/pallas_call | solution.py:153
  204.6 5.4 %collective-permute-done.9 = bf16[288,1280]{1,0:T(8,128)(2,1)S(1)} collective-permute-done((bf16[288,1280]{1,0:T(8,128)(2,1)S(1)}, bf16[288,1280]{1,0:T(8,128)(2,1)S(1)}, u32[]{:S(2)}, u32[]{:S(2)}) %collective-permute-start.9) | collective-permute-done | bytes 737312 | tf_op jit(solution)/shard_map/ppermute | solution.py:317
  210.2 1.6 collective-permute-start.13
  211.7 7.7 %down_products.11 = (bf16[288,1280]{1,0:T(8,128)(2,1)S(1)}, bf16[288,1280]{1,0:T(8,128)(2,1)S(1)}) custom-call(s32[8]{0:T(128)S(1)} %pad_add_fusion.1.blocks_ref, bf16[288,1536]{1,0:T(8,128)(2,1)S(1)} %gelu_sum.6.refs_0_, bf16[288,1024]{1,0:T(8,128)(2,1)S(1)} %gelu_sum.7.refs_1_.refs_3_, bf16[2560,10240]{1,0:T(8,128)(2,1)} %refs_2_.13, ...), custom_call_target="tpu_custom_call" | custom-call | flops 1000 | bytes 1000 | tf_op jit(solution)/shard_map/down_products/pallas_call | solution.py:153
  219.5 0.9 copy-done.4
  220.3 2.4 collective-permute-start.14
  223.0 1.1 add_convert_fusion.refs_1_
  224.1 1.1 slice.53
  225.2 1.7 collective-permute-start.12
  227.3 1.9 collective-permute-start.16
  229.2 15.9 %collective-permute-done.14.refs_3_.refs_2_ = bf16[288,1280]{1,0:T(8,128)(2,1)S(1)} collective-permute-done((bf16[288,1280]{1,0:T(8,128)(2,1)S(1)}, bf16[288,1280]{1,0:T(8,128)(2,1)S(1)}, u32[]{:S(2)}, u32[]{:S(2)}) %collective-permute-start.14) | collective-permute-done | bytes 737312 | tf_op jit(solution)/shard_map/ppermute | solution.py:348
  245.1 1.1 copy-done.2
  246.3 1.1 copy-done.5
  247.4 1.4 add_pieces.1.refs_0_
  249.0 4.2 %collective-permute-done.15.refs_1_ = bf16[288,1280]{1,0:T(8,128)(2,1)S(1)} collective-permute-done((bf16[288,1280]{1,0:T(8,128)(2,1)}, bf16[288,1280]{1,0:T(8,128)(2,1)S(1)}, u32[]{:S(2)}, u32[]{:S(2)}) %collective-permute-start.15) | collective-permute-done | bytes 737312 | tf_op jit(solution)/shard_map/ppermute | solution.py:317
  253.2 6.2 %collective-permute-done.16.refs_3_ = bf16[288,1280]{1,0:T(8,128)(2,1)S(1)} collective-permute-done((bf16[288,1280]{1,0:T(8,128)(2,1)}, bf16[288,1280]{1,0:T(8,128)(2,1)S(1)}, u32[]{:S(2)}, u32[]{:S(2)}) %collective-permute-start.16) | collective-permute-done | bytes 737312 | tf_op jit(solution)/shard_map/ppermute | solution.py:348
  259.4 1.4 finish.1
  (67 shorter events, 6.4 us)
Async XLA Ops:
  6.5 4.4 %copy-start.6 = (bf16[512,1280]{1,0:T(8,128)(2,1)S(1)}, bf16[512,1280]{1,0:T(8,128)(2,1)}, u32[]{:S(2)}) copy-start(bf16[512,1280]{1,0:T(8,128)(2,1)} %param.4) | copy-start | bytes 3932164
  6.5 8.0 %copy-start.8 = (bf16[1280]{0:T(1024)(128)(2,1)S(1)}, bf16[1280]{0:T(1024)(128)(2,1)}, u32[]{:S(2)}) copy-start(bf16[1280]{0:T(1024)(128)(2,1)} %param.5) | copy-start | bytes 7684
  6.5 55.1 %all-gather.5.cloned.1.call-start = ((), (), s32[]{:S(2)}) async-start(), calls=%async_computation.2 | async-start | bytes 2867200 | tf_op jit(solution)/shard_map/all_gather | solution.py:231
  8.6 114.8 %all-gather.3.cloned.1.call-start = ((), (), s32[]{:S(2)}) async-start(), calls=%async_computation.1 | async-start | bytes 3686400 | tf_op jit(solution)/shard_map/all_gather | solution.py:231
  10.7 213.4 %reduce-scatter.2.cloned.1.call-start = ((), (), s32[]{:S(2)}) async-start(), calls=%async_computation.3 | async-start | bytes 5734400 | tf_op jit(solution)/shard_map/reduce_scatter | solution.py:325
  11.5 4.6 %collective-permute-start = (f32[2,512]{1,0:T(2,128)S(1)}, f32[2,512]{1,0:T(2,128)S(1)}, u32[]{:S(2)}, u32[]{:S(2)}) collective-permute-start(f32[2,512]{1,0:T(2,128)S(1)} %pad_maximum_fusion.4), channel_id=1, source_target_pairs={{0,4},{4,0},{1,5},{5,1},{2,6},{6,2},{3,7},{7,3},{8,12},{12,8},{9,1... | collective-permute-start | bytes 12296 | tf_op jit(solution)/shard_map/ppermute | solution.py:246
  16.1 41.0 %collective-permute-start.3 = (f32[1,2304]{1,0:T(1,128)S(1)}, f32[1,2304]{1,0:T(1,128)S(1)}, u32[]{:S(2)}, u32[]{:S(2)}) collective-permute-start(f32[1,2304]{1,0:T(1,128)S(1)} %constant_dynamic-update-slice_fusion), channel_id=1, source_target_pairs={{0,3},{1,0},{2,1},{3,2},{4,7},{5,4},{6,5},{7,6},{8,11},{9,8},{10,9... | collective-permute-start | bytes 27656 | tf_op jit(solution)/shard_map/ppermute | solution.py:249
  55.5 4.9 %collective-permute-start.2 = (f32[1,2304]{1,0:T(1,128)S(1)}, f32[1,2304]{1,0:T(1,128)S(1)}, u32[]{:S(2)}, u32[]{:S(2)}) collective-permute-start(f32[1,2304]{1,0:T(1,128)S(1)} %constant_dynamic-update-slice_fusion), channel_id=1, source_target_pairs={{0,2},{1,3},{2,0},{3,1},{4,6},{5,7},{6,4},{7,5},{8,10},{9,11},{10,... | collective-permute-start | bytes 27656 | tf_op jit(solution)/shard_map/ppermute | solution.py:249
  55.7 5.7 %collective-permute-start.1 = (f32[1,2304]{1,0:T(1,128)S(1)}, f32[1,2304]{1,0:T(1,128)S(1)}, u32[]{:S(2)}, u32[]{:S(2)}) collective-permute-start(f32[1,2304]{1,0:T(1,128)S(1)} %constant_dynamic-update-slice_fusion), channel_id=1, source_target_pairs={{0,1},{1,2},{2,3},{3,0},{4,5},{5,6},{6,7},{7,4},{8,9},{9,10},{10,1... | collective-permute-start | bytes 27656 | tf_op jit(solution)/shard_map/ppermute | solution.py:249
  72.3 19.5 %collective-permute-start.4 = (bf16[224,1536]{1,0:T(8,128)(2,1)S(1)}, bf16[224,1536]{1,0:T(8,128)(2,1)S(1)}, u32[]{:S(2)}, u32[]{:S(2)}) collective-permute-start(bf16[224,1536]{1,0:T(8,128)(2,1)S(1)} %up_product.6.refs_0_), channel_id=1, source_target_pairs={{0,4},{4,0},{1,5},{5,1},{2,6},{6,2},{3,7},{7,3},{8,12},{12,8},{9,1... | collective-permute-start | bytes 2064392 | tf_op jit(solution)/shard_map/ppermute | solution.py:291
  79.5 19.8 %collective-permute-start.5 = (bf16[224,1024]{1,0:T(8,128)(2,1)S(1)}, bf16[224,1024]{1,0:T(8,128)(2,1)S(1)}, u32[]{:S(2)}, u32[]{:S(2)}) collective-permute-start(bf16[224,1024]{1,0:T(8,128)(2,1)S(1)} %up_product.7.refs_0_), channel_id=1, source_target_pairs={{0,4},{4,0},{1,5},{5,1},{2,6},{6,2},{3,7},{7,3},{8,12},{12,8},{9,1... | collective-permute-start | bytes 1376264 | tf_op jit(solution)/shard_map/ppermute | solution.py:291
  121.2 2.1 copy-start
  123.4 3.2 %copy-start.1 = (bf16[4,224,2560]{2,1,0:T(8,128)(2,1)S(1)}, bf16[4,224,2560]{2,1,0:T(8,128)(2,1)}, u32[]{:S(2)}) copy-start(bf16[4,224,2560]{2,1,0:T(8,128)(2,1)} %copy-done) | copy-start | bytes 13762564
  135.2 22.7 %collective-permute-start.6 = (bf16[288,1536]{1,0:T(8,128)(2,1)S(1)}, bf16[288,1536]{1,0:T(8,128)(2,1)S(1)}, u32[]{:S(2)}, u32[]{:S(2)}) collective-permute-start(bf16[288,1536]{1,0:T(8,128)(2,1)S(1)} %up_product.9.refs_0_), channel_id=1, source_target_pairs={{0,4},{4,0},{1,5},{5,1},{2,6},{6,2},{3,7},{7,3},{8,12},{12,8},{9,1... | collective-permute-start | bytes 2654216 | tf_op jit(solution)/shard_map/ppermute | solution.py:291
  142.6 25.8 %collective-permute-start.7 = (bf16[288,1024]{1,0:T(8,128)(2,1)S(1)}, bf16[288,1024]{1,0:T(8,128)(2,1)S(1)}, u32[]{:S(2)}, u32[]{:S(2)}) collective-permute-start(bf16[288,1024]{1,0:T(8,128)(2,1)S(1)} %up_product.10.refs_0_), channel_id=1, source_target_pairs={{0,4},{4,0},{1,5},{5,1},{2,6},{6,2},{3,7},{7,3},{8,12},{12,8},{9,1... | collective-permute-start | bytes 1769480 | tf_op jit(solution)/shard_map/ppermute | solution.py:291
  174.7 22.8 %collective-permute-start.8 = (bf16[288,1280]{1,0:T(8,128)(2,1)S(1)}, bf16[288,1280]{1,0:T(8,128)(2,1)S(1)}, u32[]{:S(2)}, u32[]{:S(2)}) collective-permute-start(bf16[288,1280]{1,0:T(8,128)(2,1)S(1)} %down_products.6.refs_3_), channel_id=1, source_target_pairs={{0,4},{4,0},{1,5},{5,1},{2,6},{6,2},{3,7},{7,3},{8,12},{12,8},{9,1... | collective-permute-start | bytes 2211848 | tf_op jit(solution)/shard_map/ppermute | solution.py:317
  187.5 22.4 %collective-permute-start.9 = (bf16[288,1280]{1,0:T(8,128)(2,1)S(1)}, bf16[288,1280]{1,0:T(8,128)(2,1)S(1)}, u32[]{:S(2)}, u32[]{:S(2)}) collective-permute-start(bf16[288,1280]{1,0:T(8,128)(2,1)S(1)} %down_products.8.refs_3_), channel_id=1, source_target_pairs={{0,4},{4,0},{1,5},{5,1},{2,6},{6,2},{3,7},{7,3},{8,12},{12,8},{9,1... | collective-permute-start | bytes 2211848 | tf_op jit(solution)/shard_map/ppermute | solution.py:317
  195.7 8.9 %copy-start.3 = (bf16[288,1280]{1,0:T(8,128)(2,1)}, bf16[288,1280]{1,0:T(8,128)(2,1)S(1)}, u32[]{:S(2)}) copy-start(bf16[288,1280]{1,0:T(8,128)(2,1)S(1)} %get-tuple-element.29) | copy-start | bytes 2211844
  195.7 27.3 %collective-permute-start.10 = (bf16[288,1280]{1,0:T(8,128)(2,1)S(1)}, bf16[288,1280]{1,0:T(8,128)(2,1)S(1)}, u32[]{:S(2)}, u32[]{:S(2)}) collective-permute-start(bf16[288,1280]{1,0:T(8,128)(2,1)S(1)} %get-tuple-element.25.refs_3_), channel_id=1, source_target_pairs={{0,4},{4,0},{1,5},{5,1},{2,6},{6,2},{3,7},{7,3},{8,12},{12,8},{9,1... | collective-permute-start | bytes 2211848 | tf_op jit(solution)/shard_map/ppermute | solution.py:317
  197.6 25.3 %collective-permute-start.11 = (bf16[288,1280]{1,0:T(8,128)(2,1)S(1)}, bf16[288,1280]{1,0:T(8,128)(2,1)S(1)}, u32[]{:S(2)}, u32[]{:S(2)}) collective-permute-start(bf16[288,1280]{1,0:T(8,128)(2,1)S(1)} %add_convert_fusion.2.refs_4_), channel_id=1, source_target_pairs={{0,1},{3,2},{4,5},{7,6},{8,9},{11,10},{12,13},{15,14},{16,17},{19,... | collective-permute-start | bytes 2211848 | tf_op jit(solution)/shard_map/ppermute | solution.py:342
  210.2 19.0 %collective-permute-start.13 = (bf16[288,1280]{1,0:T(8,128)(2,1)S(1)}, bf16[288,1280]{1,0:T(8,128)(2,1)}, u32[]{:S(2)}, u32[]{:S(2)}) collective-permute-start(bf16[288,1280]{1,0:T(8,128)(2,1)S(1)} %add_convert_fusion.2.refs_4_), channel_id=1, source_target_pairs={{1,2},{2,1},{5,6},{6,5},{9,10},{10,9},{13,14},{14,13},{17,18},{18,... | collective-permute-start | bytes 2211848 | tf_op jit(solution)/shard_map/ppermute | solution.py:348
  219.5 0.9 copy-start.4
  220.3 24.8 %collective-permute-start.14 = (bf16[288,1280]{1,0:T(8,128)(2,1)S(1)}, bf16[288,1280]{1,0:T(8,128)(2,1)S(1)}, u32[]{:S(2)}, u32[]{:S(2)}) collective-permute-start(bf16[288,1280]{1,0:T(8,128)(2,1)S(1)} %add_convert_fusion.1.refs_4_), channel_id=1, source_target_pairs={{0,1},{1,0},{2,3},{3,2},{4,5},{5,4},{6,7},{7,6},{8,9},{9,8},{10,11... | collective-permute-start | bytes 2211848 | tf_op jit(solution)/shard_map/ppermute | solution.py:348
  225.2 19.9 %collective-permute-start.12 = (bf16[224,1280]{1,0:T(8,128)(2,1)S(1)}, bf16[224,1280]{1,0:T(8,128)(2,1)S(1)}, u32[]{:S(2)}, u32[]{:S(2)}) collective-permute-start(bf16[224,1280]{1,0:T(8,128)(2,1)S(1)} %slice.53), channel_id=1, source_target_pairs={{0,4},{4,0},{1,5},{5,1},{2,6},{6,2},{3,7},{7,3},{8,12},{12,8},{9,1... | collective-permute-start | bytes 1720328 | tf_op jit(solution)/shard_map/ppermute | solution.py:327
  226.9 26.3 %collective-permute-start.15 = (bf16[288,1280]{1,0:T(8,128)(2,1)}, bf16[288,1280]{1,0:T(8,128)(2,1)S(1)}, u32[]{:S(2)}, u32[]{:S(2)}) collective-permute-start(bf16[288,1280]{1,0:T(8,128)(2,1)} %copy-done.3), channel_id=1, source_target_pairs={{0,4},{4,0},{1,5},{5,1},{2,6},{6,2},{3,7},{7,3},{8,12},{12,8},{9,1... | collective-permute-start | bytes 2211848 | tf_op jit(solution)/shard_map/ppermute | solution.py:317
  227.3 32.1 %collective-permute-start.16 = (bf16[288,1280]{1,0:T(8,128)(2,1)}, bf16[288,1280]{1,0:T(8,128)(2,1)S(1)}, u32[]{:S(2)}, u32[]{:S(2)}) collective-permute-start(bf16[288,1280]{1,0:T(8,128)(2,1)} %add_convert_fusion.refs_1_), channel_id=1, source_target_pairs={{0,2},{1,3},{2,0},{3,1},{4,6},{5,7},{6,4},{7,5},{8,10},{9,11},{10,... | collective-permute-start | bytes 2211848 | tf_op jit(solution)/shard_map/ppermute | solution.py:348
  245.1 1.1 copy-start.2
  246.3 1.1 copy-start.5
  247.4 1.5 copy-start.7
Sparse Core Ops, SparseCore 0:
  8.9 52.5 all-gather.4
  63.1 59.1 all-gather.2
  124.6 85.4 reduce-scatter.1
